TPU v7x, 512 devices: a whole 4x8x8 slice. The times are simulated.
512 devices in a mesh: dp: 64 (over z, y), tensor: 8 (over x, core).
Axes of the slice: x: 4, y: 8, z: 8, core: 2. Of those that a mesh axis runs over, the one named last changes fastest.
Arguments:
- queries: bfloat16 [16384, 3072], P(('dp', 'tensor')), may hold values from -16 to 16, as said below
- keys: bfloat16 [16384, 3072], P(('dp', 'tensor')), may hold values from -16 to 16
- values: bfloat16 [16384, 3072], P(('dp', 'tensor')), may hold values from -6 to 6
- out_grad: bfloat16 [16384, 3072], P(('dp', 'tensor')), may hold values from -6 to 6
- lengths: int32 [64, 32], replicated, may hold values from 5 to 8, as said below
- pack_of: int32 [64, 32], replicated, may hold values from 0 to 63, as said below
- source_ids: int32 [64, 32], replicated, may hold values from 0 to 7
- loss_weights: int32 [8], replicated, may hold values from 1 to 4
Outputs:
- grad_queries: bfloat16 [16384, 3072], P(('dp', 'tensor'))
- grad_keys: bfloat16 [16384, 3072], P(('dp', 'tensor'))
- grad_values: bfloat16 [16384, 3072], P(('dp', 'tensor'))
Inputs may be any that keep to these rules, and one draw needn't show every extreme that they name: `queries`: queries of padding rows are drawn too. `lengths`: row s lists the patch counts of the 32 images of data index s in the order of its rows. `pack_of`: no pack receives more than one image from one data index, and every pack receives exactly 32 images.
All inputs are finite; a program needn't handle non-finite values.
Results may differ from a plain program's by a relative error of at most 0.0063.
Values may be sent and summed in bfloat16 or wider, within the bound.
No kernel may reach another device: no remote copies, remote signals or barrier semaphores. Data moves between devices by JAX's collectives and lax.ppermute only.
A program may use at most 64 MiB of HBM per device.

v0:
```python
import jax
import jax.numpy as jnp
from jax import lax
from jax.sharding import PartitionSpec as P

HEAD_DIM = 128
PATCH_MAX = 8


MASKED = -1e30


def as_sent(shard):
    return jax.tree.map(lambda a: a.astype(jnp.bfloat16) if a.dtype == jnp.float32 else a, shard)


def pick_block(row_count):
    for size in (384, 256, 128):
        if row_count % size == 0:
            return size
    return row_count


def attend(queries, keys, values, grad_out, owners, row_alive):
    row_count, head_count, head_dim = queries.shape
    q_block = pick_block(row_count)
    blocks = row_count // q_block
    score_scale = HEAD_DIM ** (-0.5)
    marks = jnp.where(row_alive, owners, -1)

    def block_step(carry, block_id):
        key_acc, value_acc = carry
        allowed = (marks[:, None] == marks[None, :]) & (marks[:, None] >= 0)
        scores = (
            jnp.einsum("qhd,khd->hqk", queries, keys, preferred_element_type=jnp.float32)
            * score_scale
        )
        scores = jnp.where(allowed[None], scores, MASKED)
        row_max = jnp.max(scores, axis=-1, keepdims=True)
        exp_scores = jnp.exp(scores - row_max)
        soft_probs = exp_scores / jnp.sum(exp_scores, axis=-1, keepdims=True)
        soft_low = soft_probs.astype(jnp.bfloat16)
        attn_out = jnp.einsum("hqk,khd->qhd", soft_low, values, preferred_element_type=jnp.float32)
        row_delta = jnp.sum(grad_out.astype(jnp.float32) * attn_out, axis=-1)
        grad_values = jnp.einsum(
            "hqk,qhd->khd", soft_low, grad_out, preferred_element_type=jnp.float32
        )
        grad_probs = jnp.einsum(
            "qhd,khd->hqk", grad_out, values, preferred_element_type=jnp.float32
        )
        grad_scores = (soft_probs * (grad_probs - jnp.transpose(row_delta)[:, :, None])).astype(
            jnp.bfloat16
        )
        grad_queries = (
            jnp.einsum("hqk,khd->qhd", grad_scores, keys, preferred_element_type=jnp.float32)
            * score_scale
        )
        grad_keys = (
            jnp.einsum("hqk,qhd->khd", grad_scores, queries, preferred_element_type=jnp.float32)
            * score_scale
        )
        key_acc = key_acc + grad_keys
        value_acc = value_acc + grad_values
        return ((key_acc, value_acc), grad_queries.astype(jnp.bfloat16))

    zeros = jnp.zeros((row_count, head_count, head_dim), jnp.float32)
    (key_acc, value_acc), query_parts = lax.scan(
        block_step, (zeros, zeros), jnp.arange(blocks, dtype=jnp.int32)
    )
    grad_queries = query_parts.reshape(row_count, head_count, head_dim)
    return (grad_queries, key_acc.astype(jnp.bfloat16), value_acc.astype(jnp.bfloat16))


def image_rows(lengths_row, first_row, row_count):
    image_ends = jnp.cumsum(lengths_row)
    image_starts = image_ends - lengths_row
    row_ids = first_row + jnp.arange(row_count, dtype=jnp.int32)
    image_index = jnp.sum((row_ids[:, None] >= image_ends[None, :]).astype(jnp.int32), axis=1)
    row_alive = row_ids < image_ends[-1]
    image_index = jnp.minimum(image_index, lengths_row.shape[0] - 1)
    image_hits = image_index[:, None] == jnp.arange(lengths_row.shape[0], dtype=jnp.int32)[None, :]
    offset = row_ids - jnp.sum(jnp.where(image_hits, image_starts[None, :], 0), axis=1)
    return (image_index, image_hits, row_alive, offset)


def pair_prior(lengths, pack_of):
    image_ids = jnp.arange(lengths.shape[-1], dtype=jnp.int32)
    earlier = (pack_of[..., :, None] == pack_of[..., None, :]) & (
        image_ids[:, None] > image_ids[None, :]
    )
    return jnp.sum(jnp.where(earlier, lengths[..., None, :], 0), axis=-1)


def pack_plan(lengths, pack_of, target, row_total, capacity):
    pack_hits = pack_of == target
    incoming = jnp.sum(jnp.where(pack_hits, lengths, 0), axis=1)
    source_ends = jnp.cumsum(incoming)
    begins = source_ends - incoming
    slot_pos = jnp.arange(capacity, dtype=jnp.int32)
    live_slot = slot_pos[None, :] < incoming[:, None]
    pack_index = jnp.where(live_slot, begins[:, None] + slot_pos[None, :], row_total).reshape(-1)
    prior = pair_prior(lengths, pack_of)
    image_starts = jnp.where(pack_hits, begins[:, None] + prior, row_total).reshape(-1)
    markers = jnp.zeros((row_total,), jnp.int32).at[image_starts].add(1, mode="drop")
    owners = jnp.cumsum(markers) - 1
    pack_alive = jnp.arange(row_total, dtype=jnp.int32) < source_ends[-1]
    return (pack_index, owners, pack_alive)


def to_slots(arrays, slot_index, slot_total):
    return tuple(
        (
            jnp.zeros((slot_total,) + array.shape[1:], array.dtype)
            .at[slot_index]
            .set(array, mode="drop")
            for array in arrays
        )
    )


def compact(arrived_flat, pack_index, row_total):
    empty = jnp.zeros((row_total,) + arrived_flat.shape[1:], arrived_flat.dtype)
    return empty.at[pack_index].set(arrived_flat, mode="drop")


def local(queries, keys, values, out_grad, lengths, pack_of, source_ids, loss_weights):
    groups = lax.axis_size("dp")
    tensor_size = lax.axis_size("tensor")
    source = lax.axis_index("dp")
    tensor_rank = lax.axis_index("tensor")
    shard_rows = queries.shape[0]
    row_total = shard_rows * tensor_size
    image_count = lengths.shape[1]
    capacity = PATCH_MAX * max(1, image_count // groups)
    slot_total = groups * capacity
    lengths_row = lax.dynamic_index_in_dim(lengths, source, 0, keepdims=False)
    sources_row = lax.dynamic_index_in_dim(source_ids, source, 0, keepdims=False)
    packs_row = lax.dynamic_index_in_dim(pack_of, source, 0, keepdims=False)
    source_hits = (
        sources_row[:, None] == jnp.arange(loss_weights.shape[0], dtype=jnp.int32)[None, :]
    )
    image_weight = (
        jnp.sum(jnp.where(source_hits, loss_weights[None, :], 0), axis=1).astype(jnp.float32) * 0.25
    )
    image_index, image_hits, row_alive, offset = image_rows(
        lengths_row, tensor_rank * shard_rows, shard_rows
    )
    row_weight = jnp.where(
        row_alive, jnp.sum(jnp.where(image_hits, image_weight[None, :], 0.0), axis=1), 0.0
    )
    weighted = (out_grad.astype(jnp.float32) * row_weight[:, None]).astype(jnp.bfloat16)
    head_view = (
        lax.all_to_all(queries, "tensor", split_axis=1, concat_axis=0, tiled=True),
        lax.all_to_all(keys, "tensor", split_axis=1, concat_axis=0, tiled=True),
        lax.all_to_all(values, "tensor", split_axis=1, concat_axis=0, tiled=True),
        lax.all_to_all(weighted, "tensor", split_axis=1, concat_axis=0, tiled=True),
    )
    feat_width = head_view[0].shape[1]
    head_count = feat_width // HEAD_DIM
    image_index, image_hits, row_alive, offset = image_rows(lengths_row, 0, row_total)
    prior_row = pair_prior(lengths_row, packs_row)
    target = jnp.sum(jnp.where(image_hits, packs_row[None, :], 0), axis=1)
    row_prior = jnp.sum(jnp.where(image_hits, prior_row[None, :], 0), axis=1)
    slot_index = jnp.where(row_alive, target * capacity + row_prior + offset, slot_total)
    pack_index, owners, pack_alive = pack_plan(lengths, pack_of, source, row_total, capacity)

    def split_heads(array):
        return array.reshape(array.shape[0], head_count, HEAD_DIM)

    filled = to_slots(head_view, slot_index, slot_total)
    arrived = lax.all_to_all(
        as_sent(tuple((block.reshape(groups, capacity, feat_width) for block in filled))),
        "dp",
        split_axis=0,
        concat_axis=0,
        tiled=True,
    )
    flat = tuple(
        (compact(block.reshape(slot_total, feat_width), pack_index, row_total) for block in arrived)
    )
    grads = attend(
        split_heads(flat[0]),
        split_heads(flat[1]),
        split_heads(flat[2]),
        split_heads(flat[3]),
        owners,
        pack_alive,
    )
    packed = tuple((grad.reshape(row_total, feat_width) for grad in grads))
    returned = jax.tree.map(
        lambda part, own: part.astype(own.dtype),
        lax.all_to_all(as_sent(packed), "tensor", split_axis=0, concat_axis=1, tiled=True),
        packed,
    )
    return (returned[0], returned[1], returned[2])


def solution(mesh):
    in_specs = (
        P(("dp", "tensor"), None),
        P(("dp", "tensor"), None),
        P(("dp", "tensor"), None),
        P(("dp", "tensor"), None),
        P(),
        P(),
        P(),
        P(),
    )
    out_specs = (P(("dp", "tensor"), None), P(("dp", "tensor"), None), P(("dp", "tensor"), None))
    return jax.shard_map(local, mesh=mesh, in_specs=in_specs, out_specs=out_specs, check_vma=False)
```

profile of v0, /device:TPU:1, one launch (start us, length us, event | category | flops | bytes accessed | tf_op | source)
XLA Modules:
  0.0 190.9 jit_solution(16452705813702005074)
XLA Ops:
  4.4 1.0 multiply_convert_fusion
  6.2 10.3 %all-to-all-start.4 = ((bf16[32,8,384]{2,0,1:T(8,128)(2,1)}), bf16[32,8,384]{2,0,1:T(8,128)(2,1)S(1)}, u32[]{:S(2)}, u32[]{:S(2)}) async-start(bf16[32,8,384]{2,0,1:T(8,128)(2,1)} %bitcast.101), calls=%async_computation.4 | async-start | bytes 393216 | tf_op jit(solution)/shard_map/all_to_all | solution.py:156
  17.3 5.1 %all-to-all-done.4 = bf16[32,8,384]{2,0,1:T(8,128)(2,1)S(1)} async-done(((bf16[32,8,384]{2,0,1:T(8,128)(2,1)}), bf16[32,8,384]{2,0,1:T(8,128)(2,1)S(1)}, u32[]{:S(2)}, u32[]{:S(2)}) %all-to-all-start.4) | async-done | bytes 196640 | tf_op jit(solution)/shard_map/all_to_all | solution.py:156
  22.4 4.4 %all-to-all-start.2 = ((bf16[32,8,384]{2,0,1:T(8,128)(2,1)}), bf16[32,8,384]{2,0,1:T(8,128)(2,1)S(1)}, u32[]{:S(2)}, u32[]{:S(2)}) async-start(bf16[32,8,384]{2,0,1:T(8,128)(2,1)} %bitcast.102), calls=%async_computation.2 | async-start | bytes 393216 | tf_op jit(solution)/shard_map/all_to_all | solution.py:153
  28.7 3.9 %all-to-all-done.2 = bf16[32,8,384]{2,0,1:T(8,128)(2,1)S(1)} async-done(((bf16[32,8,384]{2,0,1:T(8,128)(2,1)}), bf16[32,8,384]{2,0,1:T(8,128)(2,1)S(1)}, u32[]{:S(2)}, u32[]{:S(2)}) %all-to-all-start.2) | async-done | bytes 196640 | tf_op jit(solution)/shard_map/all_to_all | solution.py:153
  32.7 4.2 %all-to-all-start = ((bf16[32,8,384]{2,0,1:T(8,128)(2,1)}), bf16[32,8,384]{2,0,1:T(8,128)(2,1)S(1)}, u32[]{:S(2)}, u32[]{:S(2)}) async-start(bf16[32,8,384]{2,0,1:T(8,128)(2,1)} %bitcast.103), calls=%async_computation | async-start | bytes 393216 | tf_op jit(solution)/shard_map/all_to_all | solution.py:154
  36.9 5.9 %all-to-all-done = bf16[32,8,384]{2,0,1:T(8,128)(2,1)S(1)} async-done(((bf16[32,8,384]{2,0,1:T(8,128)(2,1)}), bf16[32,8,384]{2,0,1:T(8,128)(2,1)S(1)}, u32[]{:S(2)}, u32[]{:S(2)}) %all-to-all-start) | async-done | bytes 196640 | tf_op jit(solution)/shard_map/all_to_all | solution.py:154
  42.8 4.2 %all-to-all-start.6 = ((bf16[32,8,384]{2,0,1:T(8,128)(2,1)}), bf16[32,8,384]{2,0,1:T(8,128)(2,1)S(1)}, u32[]{:S(2)}, u32[]{:S(2)}) async-start(bf16[32,8,384]{2,0,1:T(8,128)(2,1)} %bitcast.100), calls=%async_computation.6 | async-start | bytes 393216 | tf_op jit(solution)/shard_map/all_to_all | solution.py:155
  47.8 2.2 %scatter_custom_fusion.5 = bf16[512,384]{1,0:T(8,128)(2,1)} fusion(s32[256]{0:T(256)S(1)} %bitcast.149, bf16[256,384]{1,0:T(8,128)(2,1)S(1)} %bitcast.128, bf16[]{:T(256)} %constant.24.clone.1), kind=kCustom, calls=%fused_computation.47 | custom fusion | bytes 393218 | tf_op jit(solution)/shard_map/scatter | solution.py:115
  50.0 3.0 %all-to-all-done.6 = bf16[32,8,384]{2,0,1:T(8,128)(2,1)S(1)} async-done(((bf16[32,8,384]{2,0,1:T(8,128)(2,1)}), bf16[32,8,384]{2,0,1:T(8,128)(2,1)S(1)}, u32[]{:S(2)}, u32[]{:S(2)}) %all-to-all-start.6) | async-done | bytes 196640 | tf_op jit(solution)/shard_map/all_to_all | solution.py:155
  53.0 11.9 %all-to-all-start.5 = ((bf16[64,8,384]{2,1,0:T(8,128)(2,1)}), bf16[64,8,384]{2,1,0:T(8,128)(2,1)S(1)}, u32[]{:S(2)}, u32[]{:S(2)}) async-start(bf16[64,8,384]{2,1,0:T(8,128)(2,1)} %bitcast.25), calls=%async_computation.5 | async-start | bytes 786432 | tf_op jit(solution)/shard_map/all_to_all | solution.py:171
  64.9 2.2 %scatter_custom_fusion.3 = bf16[512,384]{1,0:T(8,128)(2,1)} fusion(s32[256]{0:T(256)S(1)} %bitcast.150, bf16[256,384]{1,0:T(8,128)(2,1)S(1)} %bitcast.130, bf16[]{:T(256)} %constant.24.clone.1), kind=kCustom, calls=%fused_computation.49 | custom fusion | bytes 393218 | tf_op jit(solution)/shard_map/scatter | solution.py:115
  67.1 12.0 %all-to-all-done.5 = bf16[64,8,384]{2,1,0:T(8,128)(2,1)S(1)} async-done(((bf16[64,8,384]{2,1,0:T(8,128)(2,1)}), bf16[64,8,384]{2,1,0:T(8,128)(2,1)S(1)}, u32[]{:S(2)}, u32[]{:S(2)}) %all-to-all-start.5) | async-done | bytes 393248 | tf_op jit(solution)/shard_map/all_to_all | solution.py:171
  79.1 6.8 %all-to-all-start.3 = ((bf16[64,8,384]{2,1,0:T(8,128)(2,1)}), bf16[64,8,384]{2,1,0:T(8,128)(2,1)S(1)}, u32[]{:S(2)}, u32[]{:S(2)}) async-start(bf16[64,8,384]{2,1,0:T(8,128)(2,1)} %bitcast.20), calls=%async_computation.3 | async-start | bytes 786432 | tf_op jit(solution)/shard_map/all_to_all | solution.py:171
  86.6 2.2 %scatter_custom_fusion = bf16[512,384]{1,0:T(8,128)(2,1)} fusion(s32[256]{0:T(256)S(1)} %bitcast.151, bf16[256,384]{1,0:T(8,128)(2,1)S(1)} %bitcast.129, bf16[]{:T(256)} %constant.24.clone.1), kind=kCustom, calls=%fused_computation.51 | custom fusion | bytes 393218 | tf_op jit(solution)/shard_map/scatter | solution.py:115
  88.8 11.0 %all-to-all-done.3 = bf16[64,8,384]{2,1,0:T(8,128)(2,1)S(1)} async-done(((bf16[64,8,384]{2,1,0:T(8,128)(2,1)}), bf16[64,8,384]{2,1,0:T(8,128)(2,1)S(1)}, u32[]{:S(2)}, u32[]{:S(2)}) %all-to-all-start.3) | async-done | bytes 393248 | tf_op jit(solution)/shard_map/all_to_all | solution.py:171
  99.8 6.9 %all-to-all-start.1 = ((bf16[64,8,384]{2,1,0:T(8,128)(2,1)}), bf16[64,8,384]{2,1,0:T(8,128)(2,1)S(1)}, u32[]{:S(2)}, u32[]{:S(2)}) async-start(bf16[64,8,384]{2,1,0:T(8,128)(2,1)} %bitcast.11), calls=%async_computation.1 | async-start | bytes 786432 | tf_op jit(solution)/shard_map/all_to_all | solution.py:171
  107.4 14.7 %scatter_custom_fusion.2 = s32[256]{0:T(256)S(1)} fusion(s32[2048]{0:T(1024)S(1)} %bitcast.139, s32[2048]{0:T(1024)S(1)} %broadcast.233, s32[]{:T(128)} %constant.29.clone.1), kind=kCustom, calls=%fused_computation.91 | custom fusion | flops 2048 | bytes 1028 | tf_op jit(solution)/shard_map/scatter-add | solution.py:104
  122.7 2.2 %scatter_custom_fusion.7 = bf16[512,384]{1,0:T(8,128)(2,1)} fusion(s32[256]{0:T(256)S(1)} %bitcast.152, bf16[256,384]{1,0:T(8,128)(2,1)S(1)} %bitcast.127, bf16[]{:T(256)} %constant.24.clone.1), kind=kCustom, calls=%fused_computation.45 | custom fusion | bytes 393218 | tf_op jit(solution)/shard_map/scatter | solution.py:115
  124.9 12.3 %all-to-all-start.7 = ((bf16[64,8,384]{2,1,0:T(8,128)(2,1)}), bf16[64,8,384]{2,1,0:T(8,128)(2,1)S(1)}, u32[]{:S(2)}, u32[]{:S(2)}) async-start(bf16[64,8,384]{2,1,0:T(8,128)(2,1)} %bitcast.30), calls=%async_computation.7 | async-start | bytes 786432 | tf_op jit(solution)/shard_map/all_to_all | solution.py:171
  138.2 2.4 %scatter_custom_fusion.6 = bf16[256,384]{1,0:T(8,128)(2,1)S(1)} fusion(s32[512]{0:T(512)S(1)} %bitcast.145, bf16[64,8,384]{2,1,0:T(8,128)(2,1)S(1)} %all-to-all-done.5, bf16[]{:T(256)} %constant.24.clone.1), kind=kCustom, calls=%fused_computation.31 | custom fusion | bytes 589826 | tf_op jit(solution)/shard_map/scatter | solution.py:123
  140.7 2.4 %scatter_custom_fusion.4 = bf16[256,384]{1,0:T(8,128)(2,1)S(1)} fusion(s32[512]{0:T(512)S(1)} %bitcast.146, bf16[64,8,384]{2,1,0:T(8,128)(2,1)S(1)} %all-to-all-done.3, bf16[]{:T(256)} %constant.24.clone.1), kind=kCustom, calls=%fused_computation.33 | custom fusion | bytes 589826 | tf_op jit(solution)/shard_map/scatter | solution.py:123
  143.3 2.4 %scatter_custom_fusion.1 = bf16[256,384]{1,0:T(8,128)(2,1)S(1)} fusion(s32[512]{0:T(512)S(1)} %bitcast.147, bf16[64,8,384]{2,1,0:T(8,128)(2,1)S(1)} %all-to-all-done.1, bf16[]{:T(256)} %constant.24.clone.1), kind=kCustom, calls=%fused_computation.35 | custom fusion | bytes 589826 | tf_op jit(solution)/shard_map/scatter | solution.py:123
  145.8 4.8 %all-to-all-done.7 = bf16[64,8,384]{2,1,0:T(8,128)(2,1)S(1)} async-done(((bf16[64,8,384]{2,1,0:T(8,128)(2,1)}), bf16[64,8,384]{2,1,0:T(8,128)(2,1)S(1)}, u32[]{:S(2)}, u32[]{:S(2)}) %all-to-all-start.7) | async-done | bytes 393248 | tf_op jit(solution)/shard_map/all_to_all | solution.py:171
  150.6 2.4 %scatter_custom_fusion.8 = bf16[256,384]{1,0:T(8,128)(2,1)S(1)} fusion(s32[512]{0:T(512)S(1)} %bitcast.148, bf16[64,8,384]{2,1,0:T(8,128)(2,1)S(1)} %all-to-all-done.7, bf16[]{:T(256)} %constant.24.clone.1), kind=kCustom, calls=%fused_computation.29 | custom fusion | bytes 589826 | tf_op jit(solution)/shard_map/scatter | solution.py:123
  155.9 8.0 %all-to-all-start.9 = ((bf16[8,32,384]{2,1,0:T(8,128)(2,1)}), bf16[8,32,384]{2,1,0:T(8,128)(2,1)S(1)}, u32[]{:S(2)}, u32[]{:S(2)}) async-start(bf16[8,32,384]{2,1,0:T(8,128)(2,1)} %all_to_all.134), calls=%async_computation.9 | async-start | bytes 393216 | tf_op jit(solution)/shard_map/all_to_all | solution.py:192
  164.4 0.9 all_to_all.130
  165.2 4.6 %all-to-all-done.9 = bf16[8,32,384]{2,1,0:T(8,128)(2,1)S(1)} async-done(((bf16[8,32,384]{2,1,0:T(8,128)(2,1)}), bf16[8,32,384]{2,1,0:T(8,128)(2,1)S(1)}, u32[]{:S(2)}, u32[]{:S(2)}) %all-to-all-start.9) | async-done | bytes 196640 | tf_op jit(solution)/shard_map/all_to_all | solution.py:192
  169.9 4.2 %all-to-all-start.8 = ((bf16[8,32,384]{2,1,0:T(8,128)(2,1)}), bf16[8,32,384]{2,1,0:T(8,128)(2,1)S(1)}, u32[]{:S(2)}, u32[]{:S(2)}) async-start(bf16[8,32,384]{2,1,0:T(8,128)(2,1)} %all_to_all.130), calls=%async_computation.8 | async-start | bytes 393216 | tf_op jit(solution)/shard_map/all_to_all | solution.py:192
  175.8 4.2 %all-to-all-done.8 = bf16[8,32,384]{2,1,0:T(8,128)(2,1)S(1)} async-done(((bf16[8,32,384]{2,1,0:T(8,128)(2,1)}), bf16[8,32,384]{2,1,0:T(8,128)(2,1)S(1)}, u32[]{:S(2)}, u32[]{:S(2)}) %all-to-all-start.8) | async-done | bytes 196640 | tf_op jit(solution)/shard_map/all_to_all | solution.py:192
  180.0 4.2 %all-to-all-start.10 = ((bf16[8,32,384]{2,1,0:T(8,128)(2,1)}), bf16[8,32,384]{2,1,0:T(8,128)(2,1)S(1)}, u32[]{:S(2)}, u32[]{:S(2)}) async-start(bf16[8,32,384]{2,1,0:T(8,128)(2,1)} %all_to_all.138), calls=%async_computation.10 | async-start | bytes 393216 | tf_op jit(solution)/shard_map/all_to_all | solution.py:192
  185.7 4.5 %all-to-all-done.10 = bf16[8,32,384]{2,1,0:T(8,128)(2,1)S(1)} async-done(((bf16[8,32,384]{2,1,0:T(8,128)(2,1)}), bf16[8,32,384]{2,1,0:T(8,128)(2,1)S(1)}, u32[]{:S(2)}, u32[]{:S(2)}) %all-to-all-start.10) | async-done | bytes 196640 | tf_op jit(solution)/shard_map/all_to_all | solution.py:192
  (80 shorter events, 18.2 us)
Async XLA Ops:
  1.6 0.8 copy-start.5
  1.7 0.7 copy-start
  2.6 0.7 copy-start.6
  6.1 10.4 %copy-start.1 = (bf16[32,3072]{1,0:T(8,128)(2,1)S(1)}, bf16[32,3072]{1,0:T(8,128)(2,1)}, u32[]{:S(2)}) copy-start(bf16[32,3072]{1,0:T(8,128)(2,1)} %param.8) | copy-start | bytes 589828
  6.2 16.2 %all-to-all-start.4 = ((bf16[32,8,384]{2,0,1:T(8,128)(2,1)}), bf16[32,8,384]{2,0,1:T(8,128)(2,1)S(1)}, u32[]{:S(2)}, u32[]{:S(2)}) async-start(bf16[32,8,384]{2,0,1:T(8,128)(2,1)} %bitcast.101), calls=%async_computation.4 | async-start | bytes 393216 | tf_op jit(solution)/shard_map/all_to_all | solution.py:156
  22.4 4.6 %copy-start.2 = (bf16[32,3072]{1,0:T(8,128)(2,1)S(1)}, bf16[32,3072]{1,0:T(8,128)(2,1)}, u32[]{:S(2)}) copy-start(bf16[32,3072]{1,0:T(8,128)(2,1)} %param.9) | copy-start | bytes 589828
  22.4 10.3 %all-to-all-start.2 = ((bf16[32,8,384]{2,0,1:T(8,128)(2,1)}), bf16[32,8,384]{2,0,1:T(8,128)(2,1)S(1)}, u32[]{:S(2)}, u32[]{:S(2)}) async-start(bf16[32,8,384]{2,0,1:T(8,128)(2,1)} %bitcast.102), calls=%async_computation.2 | async-start | bytes 393216 | tf_op jit(solution)/shard_map/all_to_all | solution.py:153
  26.9 1.0 copy-start.3
  32.7 10.2 %all-to-all-start = ((bf16[32,8,384]{2,0,1:T(8,128)(2,1)}), bf16[32,8,384]{2,0,1:T(8,128)(2,1)S(1)}, u32[]{:S(2)}, u32[]{:S(2)}) async-start(bf16[32,8,384]{2,0,1:T(8,128)(2,1)} %bitcast.103), calls=%async_computation | async-start | bytes 393216 | tf_op jit(solution)/shard_map/all_to_all | solution.py:154
  42.8 10.2 %all-to-all-start.6 = ((bf16[32,8,384]{2,0,1:T(8,128)(2,1)}), bf16[32,8,384]{2,0,1:T(8,128)(2,1)S(1)}, u32[]{:S(2)}, u32[]{:S(2)}) async-start(bf16[32,8,384]{2,0,1:T(8,128)(2,1)} %bitcast.100), calls=%async_computation.6 | async-start | bytes 393216 | tf_op jit(solution)/shard_map/all_to_all | solution.py:155
  53.0 26.2 %all-to-all-start.5 = ((bf16[64,8,384]{2,1,0:T(8,128)(2,1)}), bf16[64,8,384]{2,1,0:T(8,128)(2,1)S(1)}, u32[]{:S(2)}, u32[]{:S(2)}) async-start(bf16[64,8,384]{2,1,0:T(8,128)(2,1)} %bitcast.25), calls=%async_computation.5 | async-start | bytes 786432 | tf_op jit(solution)/shard_map/all_to_all | solution.py:171
  79.1 6.8 %copy-start.4 = (s32[64,32]{0,1:T(8,128)S(1)}, s32[64,32]{0,1:T(8,128)}, u32[]{:S(2)}) copy-start(s32[64,32]{0,1:T(8,128)} %param.12) | copy-start | bytes 24580
  79.1 20.6 %all-to-all-start.3 = ((bf16[64,8,384]{2,1,0:T(8,128)(2,1)}), bf16[64,8,384]{2,1,0:T(8,128)(2,1)S(1)}, u32[]{:S(2)}, u32[]{:S(2)}) async-start(bf16[64,8,384]{2,1,0:T(8,128)(2,1)} %bitcast.20), calls=%async_computation.3 | async-start | bytes 786432 | tf_op jit(solution)/shard_map/all_to_all | solution.py:171
  99.8 25.1 %all-to-all-start.1 = ((bf16[64,8,384]{2,1,0:T(8,128)(2,1)}), bf16[64,8,384]{2,1,0:T(8,128)(2,1)S(1)}, u32[]{:S(2)}, u32[]{:S(2)}) async-start(bf16[64,8,384]{2,1,0:T(8,128)(2,1)} %bitcast.11), calls=%async_computation.1 | async-start | bytes 786432 | tf_op jit(solution)/shard_map/all_to_all | solution.py:171
  124.9 25.7 %all-to-all-start.7 = ((bf16[64,8,384]{2,1,0:T(8,128)(2,1)}), bf16[64,8,384]{2,1,0:T(8,128)(2,1)S(1)}, u32[]{:S(2)}, u32[]{:S(2)}) async-start(bf16[64,8,384]{2,1,0:T(8,128)(2,1)} %bitcast.30), calls=%async_computation.7 | async-start | bytes 786432 | tf_op jit(solution)/shard_map/all_to_all | solution.py:171
  155.9 13.9 %all-to-all-start.9 = ((bf16[8,32,384]{2,1,0:T(8,128)(2,1)}), bf16[8,32,384]{2,1,0:T(8,128)(2,1)S(1)}, u32[]{:S(2)}, u32[]{:S(2)}) async-start(bf16[8,32,384]{2,1,0:T(8,128)(2,1)} %all_to_all.134), calls=%async_computation.9 | async-start | bytes 393216 | tf_op jit(solution)/shard_map/all_to_all | solution.py:192
  169.9 10.2 %all-to-all-start.8 = ((bf16[8,32,384]{2,1,0:T(8,128)(2,1)}), bf16[8,32,384]{2,1,0:T(8,128)(2,1)S(1)}, u32[]{:S(2)}, u32[]{:S(2)}) async-start(bf16[8,32,384]{2,1,0:T(8,128)(2,1)} %all_to_all.130), calls=%async_computation.8 | async-start | bytes 393216 | tf_op jit(solution)/shard_map/all_to_all | solution.py:192
  180.0 10.2 %all-to-all-start.10 = ((bf16[8,32,384]{2,1,0:T(8,128)(2,1)}), bf16[8,32,384]{2,1,0:T(8,128)(2,1)S(1)}, u32[]{:S(2)}, u32[]{:S(2)}) async-start(bf16[8,32,384]{2,1,0:T(8,128)(2,1)} %all_to_all.138), calls=%async_computation.10 | async-start | bytes 393216 | tf_op jit(solution)/shard_map/all_to_all | solution.py:192
where the time goes:
time: 192 us; the launch traced here: 191 us
  starting transfers between devices  77.6 us (40%)
  waiting for transfers between devices  59.2 us (31%)
  local copies, waits for them, and re-layouts  30.7 us (16%)
  other arithmetic  19.9 us (10%)
  matrix products  2.56 us (1%)
    all_to_all x4, starting transfers between devices, local(): lax.all_to_all(as_sent(tuple((block.reshape(groups, capacity, feat_width)...  37.9 us
    all_to_all x4, waiting for transfers between devices, local(): lax.all_to_all(as_sent(tuple((block.reshape(groups, capacity, feat_width)...  27.8 us
    all_to_all x3, starting transfers between devices, local(): lax.all_to_all(as_sent(packed), 'tensor', split_axis=0, concat_axis=1, ti...  16.5 us
    scatter-add x1, other arithmetic, pack_plan(): jnp.zeros((row_total,), jnp.int32).at[image_starts].add(1, mode='drop')  14.7 us
    all_to_all x3, waiting for transfers between devices, local(): lax.all_to_all(as_sent(packed), 'tensor', split_axis=0, concat_axis=1, ti...  13.4 us
    all_to_all x1, starting transfers between devices, local(): lax.all_to_all(weighted, 'tensor', split_axis=1, concat_axis=0, tiled=True)  10.3 us
    scatter x8, local copies, waits for them, and re-layouts, compact(): return empty.at[pack_index].set(arrived_flat, mode='drop')  10.1 us
    scatter x4, local copies, waits for them, and re-layouts, to_slots(): return tuple((jnp.zeros((slot_total,) + array.shape[1:], array.dtype).at[...  8.91 us
  transfers between devices with their start and end apart: 11, of which 10 were waited for; matrix products, arithmetic and copies ran while one was open for 21% of the time, Pallas kernels for 0%

commit v1 on v0

v1 whole, which is shorter than its diff:
```python
import jax
import jax.numpy as jnp
from jax import lax
from jax.experimental import pallas as pl
from jax.experimental.pallas import tpu as pltpu
from jax.sharding import PartitionSpec as P

HEAD_DIM = 128
PATCH_MAX = 8
MASKED = -1e30
SCALE = HEAD_DIM ** (-0.5)

NN = (((1,), (0,)), ((), ()))
NT = (((1,), (1,)), ((), ()))
TN = (((0,), (0,)), ((), ()))

STRIDE = 27
UNSTRIDE = 19

PARAMS = pltpu.CompilerParams(vmem_limit_bytes=48 * 1024 * 1024)


def dot(a, b, dims):
    return lax.dot_general(a, b, dims, preferred_element_type=jnp.float32)


def iota(shape, axis):
    return lax.broadcasted_iota(jnp.int32, shape, axis)


def low(mask):
    return mask.astype(jnp.float32).astype(jnp.bfloat16)


def split_kernel(q_ref, k_ref, v_ref, g_ref, out_ref, whole_ref, whole_sem, sem):
    ranks, _, width = out_ref.shape
    rows = q_ref.shape[0]
    whole_copies = [
        pltpu.make_async_copy(ref, whole_ref.at[at], whole_sem.at[at]) for at, ref in enumerate((q_ref, k_ref))
    ]
    copies = [
        pltpu.make_async_copy(
            ref.at[:, rank * width : (rank + 1) * width],
            out_ref.at[rank, at * rows : (at + 1) * rows, :],
            sem.at[at - 2, rank],
        )
        for at, ref in ((2, v_ref), (3, g_ref))
        for rank in range(ranks)
    ]
    for copy in whole_copies + copies:
        copy.start()
    for at, copy in enumerate(whole_copies):
        copy.wait()
        for rank in range(ranks):
            out_ref[rank, at * rows : (at + 1) * rows, :] = whole_ref[at, :, rank * width : (rank + 1) * width]
    for copy in copies:
        copy.wait()


def spread_column(column):
    return jnp.broadcast_to(column, (column.shape[0], 128)).astype(jnp.bfloat16)


def index_kernel(
    at_ref, lengths_ref, packs_ref, sources_ref, weights_ref, same_ref, scale_ref, out_place_ref, in_place_ref
):
    images, groups = lengths_ref.shape
    total = same_ref.shape[0]
    slots = groups * PATCH_MAX
    own = at_ref[0]

    lengths, packs = lengths_ref[...], packs_ref[...]
    mine = iota((images, groups), 1) == own
    lens = jnp.sum(jnp.where(mine, lengths, 0).astype(jnp.float32), axis=1, keepdims=True)
    pack = jnp.sum(jnp.where(mine, packs, 0).astype(jnp.float32), axis=1, keepdims=True)
    kind = jnp.sum(jnp.where(mine, sources_ref[...], 0).astype(jnp.float32), axis=1, keepdims=True)

    earlier = iota((images, images), 1) < iota((images, images), 0)
    lens_wide = spread_column(lens)
    starts = dot(low(earlier), lens_wide, NN)[:, 0:1]
    pack_hits = low(iota((images, groups), 1).astype(jnp.float32) == pack)
    same_pack = dot(pack_hits, pack_hits, NT) > 0.5
    prior = dot(low(same_pack & earlier), lens_wide, NN)[:, 0:1]

    row_id = iota((images, total), 1).astype(jnp.float32)
    offset = row_id - starts
    member = (offset >= 0) & (offset < lens)
    member_low = low(member)
    same_ref[...] = dot(member_low, member_low, TN).astype(jnp.bfloat16)

    weight = jnp.zeros((images, 1), jnp.float32)
    for at in range(weights_ref.shape[0]):
        weight = jnp.where(kind == at, weights_ref[at].astype(jnp.float32) * 0.25, weight)
    scale_ref[...] = dot(member_low, spread_column(weight), TN)

    place = pack * UNSTRIDE - jnp.floor(pack * (UNSTRIDE / groups)) * groups
    slot = jnp.sum(jnp.where(member, place * PATCH_MAX + prior + offset + 1.0, 0.0), axis=0, keepdims=True)
    slot = slot.astype(jnp.int32) - 1
    out_place_ref[...] = low(iota((slots, total), 0) == slot)

    arriving = jnp.where(packs == own, lengths, 0).astype(jnp.float32)
    incoming = jnp.broadcast_to(jnp.sum(arriving, axis=0, keepdims=True), (8, groups))
    before = low(iota((groups, groups), 0) < iota((groups, groups), 1))
    begins = dot(incoming.astype(jnp.bfloat16), before, NN)
    to_slots = low((iota((groups, slots), 1) // PATCH_MAX * STRIDE) % groups == iota((groups, slots), 0))
    begin_at = dot(begins.astype(jnp.bfloat16), to_slots, NN)[0:1]
    count_at = dot(incoming.astype(jnp.bfloat16), to_slots, NN)[0:1]
    within = (iota((1, slots), 1) % PATCH_MAX).astype(jnp.float32)
    row = jnp.where(within < count_at, begin_at + within, -1.0).astype(jnp.int32)
    in_place_ref[...] = low(iota((total, slots), 0) == row)


def grad_kernel(same_ref, scale_ref, place_ref, x_ref, out_ref):
    ranks, four_rows, width = x_ref.shape
    rows = four_rows // 4
    total = ranks * rows
    heads = range(width // HEAD_DIM)
    allowed = same_ref[...].astype(jnp.float32) > 0.5
    place = place_ref[...]

    def rows_of(at, head):
        cols = slice(head * HEAD_DIM, (head + 1) * HEAD_DIM)
        return x_ref[:, at * rows : (at + 1) * rows, cols].reshape(total, HEAD_DIM)

    def send(at, head, grad):
        to = at * width + head * HEAD_DIM
        out_ref[:, to : to + grad.shape[1]] = grad.astype(jnp.bfloat16)

    probs, dv = [], []
    for head in heads:
        scores = jnp.where(allowed, dot(rows_of(1, head), rows_of(0, head), NT) * SCALE, MASKED)
        exp_scores = jnp.exp(scores - jnp.max(scores, axis=0, keepdims=True))
        probs.append(exp_scores / jnp.sum(exp_scores, axis=0, keepdims=True))
    dk = []
    for head in heads:
        q, k, v = rows_of(0, head), rows_of(1, head), rows_of(2, head)
        g = (rows_of(3, head).astype(jnp.float32) * scale_ref[...]).astype(jnp.bfloat16)
        probs_low = probs[head].astype(jnp.bfloat16)
        dv.append(dot(probs_low, g, NN).astype(jnp.bfloat16))
        attn_out = dot(v, probs_low, TN)
        row_delta = jnp.sum(g.astype(jnp.float32).T * attn_out, axis=0, keepdims=True)
        grad_probs = dot(v, g, NT)
        grad_scores = (probs[head] * (grad_probs - row_delta)).astype(jnp.bfloat16)
        dk.append((dot(grad_scores, q, NN) * SCALE).astype(jnp.bfloat16))
        dq = (dot(k, grad_scores, TN) * SCALE).astype(jnp.bfloat16)
        send(0, head, dot(place, dq, NT))
    send(1, 0, dot(place, jnp.concatenate(dk, axis=1), NN))
    send(2, 0, dot(place, jnp.concatenate(dv, axis=1), NN))


def pack_kernel(place_ref, x_ref, out_ref):
    out_ref[...] = dot(place_ref[...], x_ref[...], NN).astype(jnp.bfloat16)


def join_kernel(x_ref, q_ref, k_ref, v_ref, whole_ref, sem):
    ranks, _, wide = x_ref.shape
    width = wide // 3
    copies = []
    for at, ref in enumerate((q_ref, k_ref, v_ref)):
        for rank in range(ranks):
            whole_ref[at, :, rank * width : (rank + 1) * width] = x_ref[rank, :, at * width : (at + 1) * width]
        copies.append(pltpu.make_async_copy(whole_ref.at[at], ref, sem.at[at]))
        copies[-1].start()
    for copy in copies:
        copy.wait()


def whole():
    return pl.BlockSpec(memory_space=pltpu.VMEM)


def scalars():
    return pl.BlockSpec(memory_space=pltpu.SMEM)


def in_place():
    return pl.BlockSpec(memory_space=pl.ANY)


def from_hbm(array):
    return pltpu.with_memory_space_constraint(array, pltpu.HBM)


def local(queries, keys, values, out_grad, lengths, pack_of, source_ids, loss_weights):
    groups = lax.axis_size("dp")
    ranks = lax.axis_size("tensor")
    index = lax.axis_index("dp").astype(jnp.int32).reshape(1)
    rows, feat = queries.shape
    width = feat // ranks
    total = rows * ranks
    slots = groups * PATCH_MAX
    bf16 = jnp.bfloat16

    by_rank = pl.pallas_call(
        split_kernel,
        out_shape=jax.ShapeDtypeStruct((ranks, 4 * rows, width), bf16),
        in_specs=[in_place()] * 4,
        out_specs=whole(),
        scratch_shapes=[
            pltpu.VMEM((2, rows, feat), bf16),
            pltpu.SemaphoreType.DMA((2,)),
            pltpu.SemaphoreType.DMA((2, ranks)),
        ],
        compiler_params=PARAMS,
    )(*(from_hbm(array) for array in (queries, keys, values, out_grad)))
    by_rank, index = lax.optimization_barrier((by_rank, index))
    by_head = lax.all_to_all(by_rank, "tensor", split_axis=0, concat_axis=0, tiled=True)
    same, scale, out_place, in_place_hot = pl.pallas_call(
        index_kernel,
        out_shape=(
            jax.ShapeDtypeStruct((total, total), bf16),
            jax.ShapeDtypeStruct((total, HEAD_DIM), jnp.float32),
            jax.ShapeDtypeStruct((slots, total), bf16),
            jax.ShapeDtypeStruct((total, slots), bf16),
        ),
        in_specs=[scalars(), whole(), whole(), whole(), scalars()],
        out_specs=(whole(),) * 4,
        compiler_params=PARAMS,
        cost_estimate=pl.CostEstimate(flops=1 << 24, bytes_accessed=1 << 20, transcendentals=0),
    )(index, from_hbm(lengths.T), from_hbm(pack_of.T), from_hbm(source_ids.T), loss_weights)
    in_slots = pl.pallas_call(
        grad_kernel,
        out_shape=jax.ShapeDtypeStruct((slots, 3 * width), bf16),
        in_specs=[whole()] * 4,
        out_specs=whole(),
        compiler_params=PARAMS,
    )(same, scale, out_place, by_head)
    arrived = lax.all_to_all(
        in_slots.reshape(groups, PATCH_MAX, 3 * width),
        "dp",
        split_axis=0,
        concat_axis=0,
        axis_index_groups=[[place * STRIDE % groups for place in range(groups)]],
        tiled=True,
    ).reshape(slots, 3 * width)
    packed = pl.pallas_call(
        pack_kernel,
        out_shape=jax.ShapeDtypeStruct((total, 3 * width), bf16),
        in_specs=[whole()] * 2,
        out_specs=whole(),
        compiler_params=PARAMS,
    )(in_place_hot, arrived)
    returned = lax.all_to_all(
        packed.reshape(ranks, rows, 3 * width), "tensor", split_axis=0, concat_axis=0, tiled=True
    )
    out = jax.ShapeDtypeStruct((rows, feat), bf16)
    return pl.pallas_call(
        join_kernel,
        out_shape=(out, out, out),
        in_specs=[whole()],
        out_specs=(in_place(), in_place(), in_place()),
        scratch_shapes=[pltpu.VMEM((3, rows, feat), bf16), pltpu.SemaphoreType.DMA((3,))],
        compiler_params=PARAMS,
    )(returned)


def solution(mesh):
    split = P(("dp", "tensor"), None)
    return jax.shard_map(
        local,
        mesh=mesh,
        in_specs=(split,) * 4 + (P(),) * 4,
        out_specs=(split,) * 3,
        check_vma=False,
    )
```

time: 192 us -> 86.8 us (0.45)
  starting transfers between devices: 77.6 us -> 10.3 us
  blocking collectives: 0 us -> 57.6 us
  waiting for transfers between devices: 59.2 us -> 10.8 us
  local copies, waits for them, and re-layouts: 30.7 us -> 0.01 us
  other arithmetic: 19.9 us -> 0 us
  Pallas kernels: 0 us -> 7.14 us
  matrix products: 2.56 us -> 0 us
    all_to_all x11 -> x1, starting transfers between devices: 77.6 us -> 10.3 us  [local(): lax.all_to_all(by_rank, 'tensor', split_axis=0, concat_axis=0, tiled=True)]
    all_to_all x0 -> x2, blocking collectives: none -> 57.6 us  [the longest x1 42 us: local(): lax.all_to_all(in_slots.reshape(groups, PATCH_MAX, 3 * width), 'dp', spli...]
    all_to_all x11 -> x1, waiting for transfers between devices: 59.2 us -> 10.8 us  [local(): lax.all_to_all(by_rank, 'tensor', split_axis=0, concat_axis=0, tiled=True)]
    scatter x12 -> x0, local copies, waits for them, and re-layouts: 19 us -> none  [the longest x8 10.1 us: compact(): return empty.at[pack_index].set(arrived_flat, mode='drop')]
    scatter-add x1 -> x0, other arithmetic: 14.7 us -> none  [pack_plan(): jnp.zeros((row_total,), jnp.int32).at[image_starts].add(1, mode='drop')]
    all_to_all x10 -> x0, local copies, waits for them, and re-layouts: 7.42 us -> none  [the longest x6 4.64 us: local(): lax.all_to_all(as_sent(packed), 'tensor', split_axis=0, concat_axis=1, ti...]
    pallas_call x0 -> x5, Pallas kernels: none -> 7.14 us  [the longest x1 2.31 us: local(): pl.pallas_call(split_kernel, out_shape=jax.ShapeDtypeStruct((ranks, 4 * r...]
    dot_general x5 -> x0, matrix products: 2.09 us -> none  [the longest x1 0.64 us: block_step(): jnp.einsum('hqk,khd->qhd', soft_low, values, preferred_element_type=jnp.f...]
  transfers between devices with their start and end apart: 11 -> 1, of which waited for: 10 -> 1; matrix products, arithmetic and copies ran while one was open for 21% -> 0% of each run, Pallas kernels for 0% -> 2%
where the time goes in v1:
time: 86.8 us; the launch traced here: 86.5 us
  blocking collectives  57.6 us (66%)
  waiting for transfers between devices  10.8 us (12%)
  starting transfers between devices  10.3 us (12%)
  Pallas kernels  7.14 us (8%)
    all_to_all x1, blocking collectives, local(): lax.all_to_all(in_slots.reshape(groups, PATCH_MAX, 3 * width), 'dp', spli...  42 us
    all_to_all x1, blocking collectives, local(): lax.all_to_all(packed.reshape(ranks, rows, 3 * width), 'tensor', split_ax...  15.6 us
    all_to_all x1, waiting for transfers between devices, local(): lax.all_to_all(by_rank, 'tensor', split_axis=0, concat_axis=0, tiled=True)  10.8 us
    all_to_all x1, starting transfers between devices, local(): lax.all_to_all(by_rank, 'tensor', split_axis=0, concat_axis=0, tiled=True)  10.3 us
    pallas_call x1, Pallas kernels, local(): pl.pallas_call(split_kernel, out_shape=jax.ShapeDtypeStruct((ranks, 4 * r...  2.31 us
    pallas_call x1, Pallas kernels, local(): pl.pallas_call(grad_kernel, out_shape=jax.ShapeDtypeStruct((slots, 3 * wi...  1.92 us
  transfers between devices with their start and end apart: 1, of which 1 were waited for; matrix products, arithmetic and copies ran while one was open for 0% of the time, Pallas kernels for 2%

profile of v1, /device:TPU:1, one launch (start us, length us, event | category | flops | bytes accessed | tf_op | source)
XLA Modules:
  0.0 86.5 jit_solution(12166994939590104358)
XLA Ops:
  0.6 2.3 %shard_map.103 = bf16[8,128,384]{2,1,0:T(8,128)(2,1)} custom-call(bf16[32,3072]{1,0:T(8,128)(2,1)} %q_ref.1, bf16[32,3072]{1,0:T(8,128)(2,1)} %k_ref.1, bf16[32,3072]{1,0:T(8,128)(2,1)} %v_ref.1, bf16[32,3072]{1,0:T(8,128)(2,1)} %g_ref.1), custom_call_target="tpu_custom_call" | custom-call | tf_op jit(solution)/shard_map/pallas_call | solution.py:194
  3.0 0.0 copy-start
  3.0 10.3 %all-to-all-start = ((bf16[8,128,384]{2,1,0:T(8,128)(2,1)}), bf16[8,128,384]{2,1,0:T(8,128)(2,1)S(1)}, u32[]{:S(2)}, u32[]{:S(2)}) async-start(bf16[8,128,384]{2,1,0:T(8,128)(2,1)} %shard_map.103), calls=%async_computation | async-start | bytes 1572864 | tf_op jit(solution)/shard_map/all_to_all | solution.py:207
  13.3 0.0 copy-done
  13.3 1.5 %shard_map.104 = (bf16[256,256]{1,0:T(8,128)(2,1)S(1)}, f32[256,128]{1,0:T(8,128)S(1)}, bf16[512,256]{1,0:T(8,128)(2,1)S(1)}, bf16[256,512]{1,0:T(8,128)(2,1)S(1)}) custom-call(s32[1]{0:T(128)} %bitcast.at_ref, s32[32,64]{1,0:T(8,128)} %bitcast.10, s32[32,64]{1,0:T(8,128)} %bitcast.11, s32[32,64]{1,0:T(8,128)} %bitcast.12, s32[8]{0:T(128)S(1)} %copy-done), custom_call_target="tpu_custom_call" | custom-call | flops 16777216 | bytes 1048576 | tf_op jit(solution)/shard_map/pallas_call | solution.py:208
  14.9 10.8 %all-to-all-done.x_ref = bf16[8,128,384]{2,1,0:T(8,128)(2,1)S(1)} async-done(((bf16[8,128,384]{2,1,0:T(8,128)(2,1)}), bf16[8,128,384]{2,1,0:T(8,128)(2,1)S(1)}, u32[]{:S(2)}, u32[]{:S(2)}) %all-to-all-start) | async-done | bytes 786464 | tf_op jit(solution)/shard_map/all_to_all | solution.py:207
  25.6 1.9 %shard_map.105 = bf16[512,1152]{1,0:T(8,128)(2,1)S(1)} custom-call(bf16[256,256]{1,0:T(8,128)(2,1)S(1)} %get-tuple-element.11.same_ref, f32[256,128]{1,0:T(8,128)S(1)} %get-tuple-element.12.scale_ref, bf16[512,256]{1,0:T(8,128)(2,1)S(1)} %get-tuple-element.13.place_ref, bf16[8,128,384]{2,1,0:T(8,128)(2,1)S(1)} %all-to-all-done.x_ref), custom_call_target="tpu_custom_call" | custom-call | tf_op jit(solution)/shard_map/pallas_call | solution.py:221
  27.5 42.0 %all_to_all.15 = bf16[64,8,1152]{2,1,0:T(8,128)(2,1)S(1)} all-to-all(bf16[64,8,1152]{2,1,0:T(8,128)(2,1)S(1)} %bitcast.7), channel_id=1, replica_groups={{0,216,432,136,352,56,272,488,192,408,112,328,32,248,464,168,384,88,304..., dimensions={0} | all-to-all | bytes 2359296 | tf_op jit(solution)/shard_map/all_to_all | solution.py:228
  69.5 0.5 shard_map.106
  70.1 15.6 %all_to_all.16.x_ref = bf16[8,32,1152]{2,1,0:T(8,128)(2,1)S(1)} all-to-all(bf16[8,32,1152]{2,1,0:T(8,128)(2,1)S(1)} %bitcast.9), channel_id=1, replica_groups=mesh['dp'=64,'tensor'=8] {'tensor'}, dimensions={0} | all-to-all | bytes 1179648 | tf_op jit(solution)/shard_map/all_to_all | solution.py:243
  85.6 0.8 shard_map.107
Async XLA Ops:
  3.0 10.4 %copy-start = (s32[8]{0:T(128)S(1)}, s32[8]{0:T(128)}, u32[]{:S(2)}) copy-start(s32[8]{0:T(128)} %weights_ref.1) | copy-start | bytes 100
  3.0 22.6 %all-to-all-start = ((bf16[8,128,384]{2,1,0:T(8,128)(2,1)}), bf16[8,128,384]{2,1,0:T(8,128)(2,1)S(1)}, u32[]{:S(2)}, u32[]{:S(2)}) async-start(bf16[8,128,384]{2,1,0:T(8,128)(2,1)} %shard_map.103), calls=%async_computation | async-start | bytes 1572864 | tf_op jit(solution)/shard_map/all_to_all | solution.py:207

commit v2 on v1

--- a/solution.py
+++ b/solution.py
@@ -32,9 +32,84 @@
     return mask.astype(jnp.float32).astype(jnp.bfloat16)
 
 
-def split_kernel(q_ref, k_ref, v_ref, g_ref, out_ref, whole_ref, whole_sem, sem):
+def spread_column(column):
+    return jnp.broadcast_to(column, (column.shape[0], 128)).astype(jnp.bfloat16)
+
+
+def index_work(at_ref, lengths_ref, packs_ref, sources_ref, weights_ref, same_ref, scale_ref, out_place_ref, in_place_ref):
+    images, groups = lengths_ref.shape
+    total = same_ref.shape[0]
+    slots = groups * PATCH_MAX
+    own = at_ref[0]
+
+    lengths, packs = lengths_ref[...], packs_ref[...]
+    mine = iota((images, groups), 1) == own
+    lens = jnp.sum(jnp.where(mine, lengths, 0).astype(jnp.float32), axis=1, keepdims=True)
+    pack = jnp.sum(jnp.where(mine, packs, 0).astype(jnp.float32), axis=1, keepdims=True)
+    kind = jnp.sum(jnp.where(mine, sources_ref[...], 0).astype(jnp.float32), axis=1, keepdims=True)
+
+    earlier = iota((images, images), 1) < iota((images, images), 0)
+    lens_wide = spread_column(lens)
+    starts = dot(low(earlier), lens_wide, NN)[:, 0:1]
+    pack_hits = low(iota((images, groups), 1).astype(jnp.float32) == pack)
+    same_pack = dot(pack_hits, pack_hits, NT) > 0.5
+    prior = dot(low(same_pack & earlier), lens_wide, NN)[:, 0:1]
+
+    row_id = iota((images, total), 1).astype(jnp.float32)
+    offset = row_id - starts
+    member = (offset >= 0) & (offset < lens)
+    member_low = low(member)
+    same_ref[...] = dot(member_low, member_low, TN).astype(jnp.bfloat16)
+
+    weight = jnp.zeros((images, 1), jnp.float32)
+    for at in range(weights_ref.shape[0]):
+        weight = jnp.where(kind == at, weights_ref[at].astype(jnp.float32) * 0.25, weight)
+    scale_ref[...] = dot(member_low, spread_column(weight), TN)
+
+    place = pack * UNSTRIDE - jnp.floor(pack * (UNSTRIDE / groups)) * groups
+    slot = jnp.sum(jnp.where(member, place * PATCH_MAX + prior + offset + 1.0, 0.0), axis=0, keepdims=True)
+    slot = slot.astype(jnp.int32) - 1
+    out_place_ref[...] = low(iota((slots, total), 0) == slot)
+
+    arriving = jnp.where(packs == own, lengths, 0).astype(jnp.float32)
+    incoming = jnp.broadcast_to(jnp.sum(arriving, axis=0, keepdims=True), (8, groups))
+    before = low(iota((groups, groups), 0) < iota((groups, groups), 1))
+    begins = dot(incoming.astype(jnp.bfloat16), before, NN)
+    to_slots = low((iota((groups, slots), 1) // PATCH_MAX * STRIDE) % groups == iota((groups, slots), 0))
+    begin_at = dot(begins.astype(jnp.bfloat16), to_slots, NN)[0:1]
+    count_at = dot(incoming.astype(jnp.bfloat16), to_slots, NN)[0:1]
+    within = (iota((1, slots), 1) % PATCH_MAX).astype(jnp.float32)
+    row = jnp.where(within < count_at, begin_at + within, -1.0).astype(jnp.int32)
+    in_place_ref[...] = low(iota((total, slots), 0) == row)
+
+
+def split_kernel(
+    at_ref,
+    weights_ref,
+    lengths_hbm,
+    packs_hbm,
+    sources_hbm,
+    q_ref,
+    k_ref,
+    v_ref,
+    g_ref,
+    out_ref,
+    same_ref,
+    scale_ref,
+    out_place_ref,
+    in_place_ref,
+    number_ref,
+    whole_ref,
+    number_sem,
+    whole_sem,
+    sem,
+):
     ranks, _, width = out_ref.shape
     rows = q_ref.shape[0]
+    number_copies = [
+        pltpu.make_async_copy(ref, number_ref.at[at], number_sem.at[at])
+        for at, ref in enumerate((lengths_hbm, packs_hbm, sources_hbm))
+    ]
     whole_copies = [
         pltpu.make_async_copy(ref, whole_ref.at[at], whole_sem.at[at]) for at, ref in enumerate((q_ref, k_ref))
     ]
@@ -47,67 +122,27 @@
         for at, ref in ((2, v_ref), (3, g_ref))
         for rank in range(ranks)
     ]
-    for copy in whole_copies + copies:
+    for copy in number_copies + whole_copies + copies:
         copy.start()
+    for copy in number_copies:
+        copy.wait()
+    index_work(
+        at_ref,
+        number_ref.at[0],
+        number_ref.at[1],
+        number_ref.at[2],
+        weights_ref,
+        same_ref,
+        scale_ref,
+        out_place_ref,
+        in_place_ref,
+    )
     for at, copy in enumerate(whole_copies):
         copy.wait()
         for rank in range(ranks):
             out_ref[rank, at * rows : (at + 1) * rows, :] = whole_ref[at, :, rank * width : (rank + 1) * width]
     for copy in copies:
         copy.wait()
-
-
-def spread_column(column):
-    return jnp.broadcast_to(column, (column.shape[0], 128)).astype(jnp.bfloat16)
-
-
-def index_kernel(
-    at_ref, lengths_ref, packs_ref, sources_ref, weights_ref, same_ref, scale_ref, out_place_ref, in_place_ref
-):
-    images, groups = lengths_ref.shape
-    total = same_ref.shape[0]
-    slots = groups * PATCH_MAX
-    own = at_ref[0]
-
-    lengths, packs = lengths_ref[...], packs_ref[...]
-    mine = iota((images, groups), 1) == own
-    lens = jnp.sum(jnp.where(mine, lengths, 0).astype(jnp.float32), axis=1, keepdims=True)
-    pack = jnp.sum(jnp.where(mine, packs, 0).astype(jnp.float32), axis=1, keepdims=True)
-    kind = jnp.sum(jnp.where(mine, sources_ref[...], 0).astype(jnp.float32), axis=1, keepdims=True)
-
-    earlier = iota((images, images), 1) < iota((images, images), 0)
-    lens_wide = spread_column(lens)
-    starts = dot(low(earlier), lens_wide, NN)[:, 0:1]
-    pack_hits = low(iota((images, groups), 1).astype(jnp.float32) == pack)
-    same_pack = dot(pack_hits, pack_hits, NT) > 0.5
-    prior = dot(low(same_pack & earlier), lens_wide, NN)[:, 0:1]
-
-    row_id = iota((images, total), 1).astype(jnp.float32)
-    offset = row_id - starts
-    member = (offset >= 0) & (offset < lens)
-    member_low = low(member)
-    same_ref[...] = dot(member_low, member_low, TN).astype(jnp.bfloat16)
-
-    weight = jnp.zeros((images, 1), jnp.float32)
-    for at in range(weights_ref.shape[0]):
-        weight = jnp.where(kind == at, weights_ref[at].astype(jnp.float32) * 0.25, weight)
-    scale_ref[...] = dot(member_low, spread_column(weight), TN)
-
-    place = pack * UNSTRIDE - jnp.floor(pack * (UNSTRIDE / groups)) * groups
-    slot = jnp.sum(jnp.where(member, place * PATCH_MAX + prior + offset + 1.0, 0.0), axis=0, keepdims=True)
-    slot = slot.astype(jnp.int32) - 1
-    out_place_ref[...] = low(iota((slots, total), 0) == slot)
-
-    arriving = jnp.where(packs == own, lengths, 0).astype(jnp.float32)
-    incoming = jnp.broadcast_to(jnp.sum(arriving, axis=0, keepdims=True), (8, groups))
-    before = low(iota((groups, groups), 0) < iota((groups, groups), 1))
-    begins = dot(incoming.astype(jnp.bfloat16), before, NN)
-    to_slots = low((iota((groups, slots), 1) // PATCH_MAX * STRIDE) % groups == iota((groups, slots), 0))
-    begin_at = dot(begins.astype(jnp.bfloat16), to_slots, NN)[0:1]
-    count_at = dot(incoming.astype(jnp.bfloat16), to_slots, NN)[0:1]
-    within = (iota((1, slots), 1) % PATCH_MAX).astype(jnp.float32)
-    row = jnp.where(within < count_at, begin_at + within, -1.0).astype(jnp.int32)
-    in_place_ref[...] = low(iota((total, slots), 0) == row)
 
 
 def grad_kernel(same_ref, scale_ref, place_ref, x_ref, out_ref):
@@ -191,33 +226,28 @@
     slots = groups * PATCH_MAX
     bf16 = jnp.bfloat16
 
-    by_rank = pl.pallas_call(
+    numbers = (lengths.T, pack_of.T, source_ids.T)
+    by_rank, same, scale, out_place, in_place_hot = pl.pallas_call(
         split_kernel,
-        out_shape=jax.ShapeDtypeStruct((ranks, 4 * rows, width), bf16),
-        in_specs=[in_place()] * 4,
-        out_specs=whole(),
-        scratch_shapes=[
-            pltpu.VMEM((2, rows, feat), bf16),
-            pltpu.SemaphoreType.DMA((2,)),
-            pltpu.SemaphoreType.DMA((2, ranks)),
-        ],
-        compiler_params=PARAMS,
-    )(*(from_hbm(array) for array in (queries, keys, values, out_grad)))
-    by_rank, index = lax.optimization_barrier((by_rank, index))
-    by_head = lax.all_to_all(by_rank, "tensor", split_axis=0, concat_axis=0, tiled=True)
-    same, scale, out_place, in_place_hot = pl.pallas_call(
-        index_kernel,
         out_shape=(
+            jax.ShapeDtypeStruct((ranks, 4 * rows, width), bf16),
             jax.ShapeDtypeStruct((total, total), bf16),
             jax.ShapeDtypeStruct((total, HEAD_DIM), jnp.float32),
             jax.ShapeDtypeStruct((slots, total), bf16),
             jax.ShapeDtypeStruct((total, slots), bf16),
         ),
-        in_specs=[scalars(), whole(), whole(), whole(), scalars()],
-        out_specs=(whole(),) * 4,
-        compiler_params=PARAMS,
-        cost_estimate=pl.CostEstimate(flops=1 << 24, bytes_accessed=1 << 20, transcendentals=0),
-    )(index, from_hbm(lengths.T), from_hbm(pack_of.T), from_hbm(source_ids.T), loss_weights)
+        in_specs=[scalars(), scalars()] + [in_place()] * 7,
+        out_specs=(whole(),) * 5,
+        scratch_shapes=[
+            pltpu.VMEM((3,) + numbers[0].shape, jnp.int32),
+            pltpu.VMEM((2, rows, feat), bf16),
+            pltpu.SemaphoreType.DMA((3,)),
+            pltpu.SemaphoreType.DMA((2,)),
+            pltpu.SemaphoreType.DMA((2, ranks)),
+        ],
+        compiler_params=PARAMS,
+    )(index, *(from_hbm(array) for array in (loss_weights,) + numbers + (queries, keys, values, out_grad)))
+    by_head = lax.all_to_all(by_rank, "tensor", split_axis=0, concat_axis=0, tiled=True)
     in_slots = pl.pallas_call(
         grad_kernel,
         out_shape=jax.ShapeDtypeStruct((slots, 3 * width), bf16),

time: 86.8 us -> 87.1 us (level)
  blocking collectives: 57.6 us -> 80.2 us
  waiting for transfers between devices: 10.8 us -> 0 us
  starting transfers between devices: 10.3 us -> 0 us
  Pallas kernels: 7.14 us -> 6 us
    all_to_all x0 -> x1, blocking collectives: none -> 21.5 us  [local(): lax.all_to_all(by_rank, 'tensor', split_axis=0, concat_axis=0, tiled=True)]
    all_to_all x1 -> x0, waiting for transfers between devices: 10.8 us -> none  [local(): lax.all_to_all(by_rank, 'tensor', split_axis=0, concat_axis=0, tiled=True)]
    all_to_all x1 -> x0, starting transfers between devices: 10.3 us -> none  [local(): lax.all_to_all(by_rank, 'tensor', split_axis=0, concat_axis=0, tiled=True)]
    pallas_call x2 -> x1, Pallas kernels: 3.86 us -> 2.72 us  [local(): pl.pallas_call(split_kernel, out_shape=(jax.ShapeDtypeStruct((ranks, 4 *...]
  transfers between devices with their start and end apart: 1 -> 0, of which waited for: 1 -> 0; matrix products, arithmetic and copies ran while one was open for 0% -> 0% of each run, Pallas kernels for 2% -> 0%
where the time goes in v2:
time: 87.1 us; the launch traced here: 86.9 us
  blocking collectives  80.2 us (92%)
  Pallas kernels  6 us (7%)
    all_to_all x1, blocking collectives, local(): lax.all_to_all(in_slots.reshape(groups, PATCH_MAX, 3 * width), 'dp', spli...  42.6 us
    all_to_all x1, blocking collectives, local(): lax.all_to_all(by_rank, 'tensor', split_axis=0, concat_axis=0, tiled=True)  21.5 us
    all_to_all x1, blocking collectives, local(): lax.all_to_all(packed.reshape(ranks, rows, 3 * width), 'tensor', split_ax...  16.1 us
    pallas_call x1, Pallas kernels, local(): pl.pallas_call(split_kernel, out_shape=(jax.ShapeDtypeStruct((ranks, 4 *...  2.72 us
    pallas_call x1, Pallas kernels, local(): pl.pallas_call(grad_kernel, out_shape=jax.ShapeDtypeStruct((slots, 3 * wi...  1.93 us

profile of v2, /device:TPU:1, one launch (start us, length us, event | category | flops | bytes accessed | tf_op | source)
XLA Modules:
  0.0 86.9 jit_solution(1107275185060103054)
XLA Ops:
  0.6 2.7 %shard_map.103 = (bf16[8,128,384]{2,1,0:T(8,128)(2,1)S(1)}, bf16[256,256]{1,0:T(8,128)(2,1)S(1)}, f32[256,128]{1,0:T(8,128)S(1)}, bf16[512,256]{1,0:T(8,128)(2,1)S(1)}, bf16[256,512]{1,0:T(8,128)(2,1)S(1)}) custom-call(s32[1]{0:T(128)} %bitcast.at_ref, s32[8]{0:T(128)} %weights_ref.1, s32[32,64]{1,0:T(8,128)} %bitcast.10, s32[32,64]{1,0:T(8,128)} %bitcast.11, ...), custom_call_target="tpu_custom_call" | custom-call | tf_op jit(solution)/shard_map/pallas_call | solution.py:230
  3.4 21.5 %all_to_all.15.x_ref = bf16[8,128,384]{2,1,0:T(8,128)(2,1)S(1)} all-to-all(bf16[8,128,384]{2,1,0:T(8,128)(2,1)S(1)} %get-tuple-element.12), channel_id=1, replica_groups=mesh['dp'=64,'tensor'=8] {'tensor'}, dimensions={0} | all-to-all | bytes 1572864 | tf_op jit(solution)/shard_map/all_to_all | solution.py:250
  24.9 1.9 %shard_map.104 = bf16[512,1152]{1,0:T(8,128)(2,1)S(1)} custom-call(bf16[256,256]{1,0:T(8,128)(2,1)S(1)} %get-tuple-element.9.same_ref, f32[256,128]{1,0:T(8,128)S(1)} %get-tuple-element.10.scale_ref, bf16[512,256]{1,0:T(8,128)(2,1)S(1)} %get-tuple-element.11.place_ref, bf16[8,128,384]{2,1,0:T(8,128)(2,1)S(1)} %all_to_all.15.x_ref), custom_call_target="tpu_custom_call" | custom-call | tf_op jit(solution)/shard_map/pallas_call | solution.py:251
  26.8 42.6 %all_to_all.16 = bf16[64,8,1152]{2,1,0:T(8,128)(2,1)S(1)} all-to-all(bf16[64,8,1152]{2,1,0:T(8,128)(2,1)S(1)} %bitcast.7), channel_id=1, replica_groups={{0,216,432,136,352,56,272,488,192,408,112,328,32,248,464,168,384,88,304..., dimensions={0} | all-to-all | bytes 2359296 | tf_op jit(solution)/shard_map/all_to_all | solution.py:258
  69.4 0.5 shard_map.105
  69.9 16.1 %all_to_all.17.x_ref = bf16[8,32,1152]{2,1,0:T(8,128)(2,1)S(1)} all-to-all(bf16[8,32,1152]{2,1,0:T(8,128)(2,1)S(1)} %bitcast.9), channel_id=1, replica_groups=mesh['dp'=64,'tensor'=8] {'tensor'}, dimensions={0} | all-to-all | bytes 1179648 | tf_op jit(solution)/shard_map/all_to_all | solution.py:273
  86.0 0.8 shard_map.106

commit v3 on v1

--- a/solution.py
+++ b/solution.py
@@ -9,6 +9,7 @@
 PATCH_MAX = 8
 MASKED = -1e30
 SCALE = HEAD_DIM ** (-0.5)
+SCALE_BASE2 = SCALE * 1.4426950408889634
 
 NN = (((1,), (0,)), ((), ()))
 NT = (((1,), (1,)), ((), ()))
@@ -32,7 +33,7 @@
     return mask.astype(jnp.float32).astype(jnp.bfloat16)
 
 
-def split_kernel(q_ref, k_ref, v_ref, g_ref, out_ref, whole_ref, whole_sem, sem):
+def split_kernel(q_ref, k_ref, v_ref, g_ref, out_ref, whole_ref, built_ref, whole_sem, sem, out_sem):
     ranks, _, width = out_ref.shape
     rows = q_ref.shape[0]
     whole_copies = [
@@ -41,7 +42,7 @@
     copies = [
         pltpu.make_async_copy(
             ref.at[:, rank * width : (rank + 1) * width],
-            out_ref.at[rank, at * rows : (at + 1) * rows, :],
+            built_ref.at[rank, at * rows : (at + 1) * rows, :],
             sem.at[at - 2, rank],
         )
         for at, ref in ((2, v_ref), (3, g_ref))
@@ -52,8 +53,20 @@
     for at, copy in enumerate(whole_copies):
         copy.wait()
         for rank in range(ranks):
-            out_ref[rank, at * rows : (at + 1) * rows, :] = whole_ref[at, :, rank * width : (rank + 1) * width]
+            built_ref[rank, at * rows : (at + 1) * rows, :] = whole_ref[at, :, rank * width : (rank + 1) * width]
+    halves = [
+        pltpu.make_async_copy(
+            built_ref.at[:, half * rows : (half + 2) * rows, :],
+            out_ref.at[:, half * rows : (half + 2) * rows, :],
+            out_sem.at[half // 2],
+        )
+        for half in (0, 2)
+    ]
+    halves[0].start()
     for copy in copies:
+        copy.wait()
+    halves[1].start()
+    for copy in halves:
         copy.wait()
 
 
@@ -86,7 +99,7 @@
     offset = row_id - starts
     member = (offset >= 0) & (offset < lens)
     member_low = low(member)
-    same_ref[...] = dot(member_low, member_low, TN).astype(jnp.bfloat16)
+    same_ref[...] = jnp.where(dot(member_low, member_low, TN) > 0.5, 0.0, MASKED)
 
     weight = jnp.zeros((images, 1), jnp.float32)
     for at in range(weights_ref.shape[0]):
@@ -115,37 +128,34 @@
     rows = four_rows // 4
     total = ranks * rows
     heads = range(width // HEAD_DIM)
-    allowed = same_ref[...].astype(jnp.float32) > 0.5
+    mask = same_ref[...]
     place = place_ref[...]
 
     def rows_of(at, head):
         cols = slice(head * HEAD_DIM, (head + 1) * HEAD_DIM)
         return x_ref[:, at * rows : (at + 1) * rows, cols].reshape(total, HEAD_DIM)
 
-    def send(at, head, grad):
-        to = at * width + head * HEAD_DIM
-        out_ref[:, to : to + grad.shape[1]] = grad.astype(jnp.bfloat16)
-
-    probs, dv = [], []
+    def send(at, product):
+        out_ref[:, at * width : (at + 1) * width] = product.astype(jnp.bfloat16)
+
+    probs, grad_probs, dv = [], [], []
     for head in heads:
-        scores = jnp.where(allowed, dot(rows_of(1, head), rows_of(0, head), NT) * SCALE, MASKED)
-        exp_scores = jnp.exp(scores - jnp.max(scores, axis=0, keepdims=True))
-        probs.append(exp_scores / jnp.sum(exp_scores, axis=0, keepdims=True))
-    dk = []
+        scores = dot(rows_of(1, head), rows_of(0, head), NT) * SCALE_BASE2 + mask
+        exp_scores = jnp.exp2(scores - jnp.max(scores, axis=0, keepdims=True))
+        probs.append(exp_scores * (1.0 / jnp.sum(exp_scores, axis=0, keepdims=True)))
+        g = (rows_of(3, head).astype(jnp.float32) * scale_ref[...]).astype(jnp.bfloat16)
+        grad_probs.append(dot(rows_of(2, head), g, NT))
+        dv.append(dot(probs[head].astype(jnp.bfloat16), g, NN).astype(jnp.bfloat16))
+    dq, dk = [], []
     for head in heads:
-        q, k, v = rows_of(0, head), rows_of(1, head), rows_of(2, head)
-        g = (rows_of(3, head).astype(jnp.float32) * scale_ref[...]).astype(jnp.bfloat16)
-        probs_low = probs[head].astype(jnp.bfloat16)
-        dv.append(dot(probs_low, g, NN).astype(jnp.bfloat16))
-        attn_out = dot(v, probs_low, TN)
-        row_delta = jnp.sum(g.astype(jnp.float32).T * attn_out, axis=0, keepdims=True)
-        grad_probs = dot(v, g, NT)
-        grad_scores = (probs[head] * (grad_probs - row_delta)).astype(jnp.bfloat16)
-        dk.append((dot(grad_scores, q, NN) * SCALE).astype(jnp.bfloat16))
-        dq = (dot(k, grad_scores, TN) * SCALE).astype(jnp.bfloat16)
-        send(0, head, dot(place, dq, NT))
-    send(1, 0, dot(place, jnp.concatenate(dk, axis=1), NN))
-    send(2, 0, dot(place, jnp.concatenate(dv, axis=1), NN))
+        probs_low = probs[head].astype(jnp.bfloat16).astype(jnp.float32)
+        row_delta = jnp.sum(probs_low * grad_probs[head], axis=0, keepdims=True)
+        grad_scores = (probs[head] * (grad_probs[head] - row_delta)).astype(jnp.bfloat16)
+        dk.append((dot(grad_scores, rows_of(0, head), NN) * SCALE).astype(jnp.bfloat16))
+        dq.append((dot(rows_of(1, head), grad_scores, TN) * SCALE).astype(jnp.bfloat16))
+    send(2, dot(place, jnp.concatenate(dv, axis=1), NN))
+    send(1, dot(place, jnp.concatenate(dk, axis=1), NN))
+    send(0, dot(place, jnp.concatenate(dq, axis=0), NT))
 
 
 def pack_kernel(place_ref, x_ref, out_ref):
@@ -195,11 +205,13 @@
         split_kernel,
         out_shape=jax.ShapeDtypeStruct((ranks, 4 * rows, width), bf16),
         in_specs=[in_place()] * 4,
-        out_specs=whole(),
+        out_specs=in_place(),
         scratch_shapes=[
             pltpu.VMEM((2, rows, feat), bf16),
+            pltpu.VMEM((ranks, 4 * rows, width), bf16),
             pltpu.SemaphoreType.DMA((2,)),
             pltpu.SemaphoreType.DMA((2, ranks)),
+            pltpu.SemaphoreType.DMA((2,)),
         ],
         compiler_params=PARAMS,
     )(*(from_hbm(array) for array in (queries, keys, values, out_grad)))
@@ -208,7 +220,7 @@
     same, scale, out_place, in_place_hot = pl.pallas_call(
         index_kernel,
         out_shape=(
-            jax.ShapeDtypeStruct((total, total), bf16),
+            jax.ShapeDtypeStruct((total, total), jnp.float32),
             jax.ShapeDtypeStruct((total, HEAD_DIM), jnp.float32),
             jax.ShapeDtypeStruct((slots, total), bf16),
             jax.ShapeDtypeStruct((total, slots), bf16),

time: 86.8 us -> 86.4 us (level)
  no operation moved by 1% of the time
where the time goes in v3:
time: 86.4 us; the launch traced here: 86 us
  blocking collectives  57.6 us (67%)
  waiting for transfers between devices  10.8 us (12%)
  starting transfers between devices  10.3 us (12%)
  Pallas kernels  6.69 us (8%)
    all_to_all x1, blocking collectives, local(): lax.all_to_all(in_slots.reshape(groups, PATCH_MAX, 3 * width), 'dp', spli...  42 us
    all_to_all x1, blocking collectives, local(): lax.all_to_all(packed.reshape(ranks, rows, 3 * width), 'tensor', split_ax...  15.5 us
    all_to_all x1, waiting for transfers between devices, local(): lax.all_to_all(by_rank, 'tensor', split_axis=0, concat_axis=0, tiled=True)  10.8 us
    all_to_all x1, starting transfers between devices, local(): lax.all_to_all(by_rank, 'tensor', split_axis=0, concat_axis=0, tiled=True)  10.3 us
    pallas_call x1, Pallas kernels, local(): pl.pallas_call(split_kernel, out_shape=jax.ShapeDtypeStruct((ranks, 4 * r...  2.31 us
  transfers between devices with their start and end apart: 1, of which 1 were waited for; matrix products, arithmetic and copies ran while one was open for 0% of the time, Pallas kernels for 2%

profile of v3, /device:TPU:1, one launch (start us, length us, event | category | flops | bytes accessed | tf_op | source)
XLA Modules:
  0.0 86.0 jit_solution(14814850526702268392)
XLA Ops:
  0.6 2.3 %shard_map.103 = bf16[8,128,384]{2,1,0:T(8,128)(2,1)} custom-call(bf16[32,3072]{1,0:T(8,128)(2,1)} %q_ref.1, bf16[32,3072]{1,0:T(8,128)(2,1)} %k_ref.1, bf16[32,3072]{1,0:T(8,128)(2,1)} %v_ref.1, bf16[32,3072]{1,0:T(8,128)(2,1)} %g_ref.1), custom_call_target="tpu_custom_call" | custom-call | tf_op jit(solution)/shard_map/pallas_call | solution.py:204
  3.0 0.0 copy-start
  3.0 10.3 %all-to-all-start = ((bf16[8,128,384]{2,1,0:T(8,128)(2,1)}), bf16[8,128,384]{2,1,0:T(8,128)(2,1)S(1)}, u32[]{:S(2)}, u32[]{:S(2)}) async-start(bf16[8,128,384]{2,1,0:T(8,128)(2,1)} %shard_map.103), calls=%async_computation | async-start | bytes 1572864 | tf_op jit(solution)/shard_map/all_to_all | solution.py:219
  13.3 0.0 copy-done
  13.3 1.6 %shard_map.104 = (f32[256,256]{1,0:T(8,128)S(1)}, f32[256,128]{1,0:T(8,128)S(1)}, bf16[512,256]{1,0:T(8,128)(2,1)S(1)}, bf16[256,512]{1,0:T(8,128)(2,1)S(1)}) custom-call(s32[1]{0:T(128)} %bitcast.at_ref, s32[32,64]{1,0:T(8,128)} %bitcast.10, s32[32,64]{1,0:T(8,128)} %bitcast.11, s32[32,64]{1,0:T(8,128)} %bitcast.12, s32[8]{0:T(128)S(1)} %copy-done), custom_call_target="tpu_custom_call" | custom-call | flops 16777216 | bytes 1048576 | tf_op jit(solution)/shard_map/pallas_call | solution.py:220
  14.9 10.8 %all-to-all-done.x_ref = bf16[8,128,384]{2,1,0:T(8,128)(2,1)S(1)} async-done(((bf16[8,128,384]{2,1,0:T(8,128)(2,1)}), bf16[8,128,384]{2,1,0:T(8,128)(2,1)S(1)}, u32[]{:S(2)}, u32[]{:S(2)}) %all-to-all-start) | async-done | bytes 786464 | tf_op jit(solution)/shard_map/all_to_all | solution.py:219
  25.6 1.5 %shard_map.105 = bf16[512,1152]{1,0:T(8,128)(2,1)S(1)} custom-call(f32[256,256]{1,0:T(8,128)S(1)} %get-tuple-element.11.same_ref, f32[256,128]{1,0:T(8,128)S(1)} %get-tuple-element.12.scale_ref, bf16[512,256]{1,0:T(8,128)(2,1)S(1)} %get-tuple-element.13.place_ref, bf16[8,128,384]{2,1,0:T(8,128)(2,1)S(1)} %all-to-all-done.x_ref), custom_call_target="tpu_custom_call" | custom-call | tf_op jit(solution)/shard_map/pallas_call | solution.py:233
  27.1 42.0 %all_to_all.15 = bf16[64,8,1152]{2,1,0:T(8,128)(2,1)S(1)} all-to-all(bf16[64,8,1152]{2,1,0:T(8,128)(2,1)S(1)} %bitcast.7), channel_id=1, replica_groups={{0,216,432,136,352,56,272,488,192,408,112,328,32,248,464,168,384,88,304..., dimensions={0} | all-to-all | bytes 2359296 | tf_op jit(solution)/shard_map/all_to_all | solution.py:240
  69.1 0.5 shard_map.106
  69.6 15.5 %all_to_all.16.x_ref = bf16[8,32,1152]{2,1,0:T(8,128)(2,1)S(1)} all-to-all(bf16[8,32,1152]{2,1,0:T(8,128)(2,1)S(1)} %bitcast.9), channel_id=1, replica_groups=mesh['dp'=64,'tensor'=8] {'tensor'}, dimensions={0} | all-to-all | bytes 1179648 | tf_op jit(solution)/shard_map/all_to_all | solution.py:255
  85.2 0.8 shard_map.107
Async XLA Ops:
  3.0 10.4 %copy-start = (s32[8]{0:T(128)S(1)}, s32[8]{0:T(128)}, u32[]{:S(2)}) copy-start(s32[8]{0:T(128)} %weights_ref.1) | copy-start | bytes 100
  3.0 22.6 %all-to-all-start = ((bf16[8,128,384]{2,1,0:T(8,128)(2,1)}), bf16[8,128,384]{2,1,0:T(8,128)(2,1)S(1)}, u32[]{:S(2)}, u32[]{:S(2)}) async-start(bf16[8,128,384]{2,1,0:T(8,128)(2,1)} %shard_map.103), calls=%async_computation | async-start | bytes 1572864 | tf_op jit(solution)/shard_map/all_to_all | solution.py:219

commit v4 on v3

--- a/solution.py
+++ b/solution.py
@@ -33,7 +33,7 @@
     return mask.astype(jnp.float32).astype(jnp.bfloat16)
 
 
-def split_kernel(q_ref, k_ref, v_ref, g_ref, out_ref, whole_ref, built_ref, whole_sem, sem, out_sem):
+def split_kernel(q_ref, k_ref, v_ref, g_ref, out_ref, whole_ref, whole_sem, sem):
     ranks, _, width = out_ref.shape
     rows = q_ref.shape[0]
     whole_copies = [
@@ -42,7 +42,7 @@
     copies = [
         pltpu.make_async_copy(
             ref.at[:, rank * width : (rank + 1) * width],
-            built_ref.at[rank, at * rows : (at + 1) * rows, :],
+            out_ref.at[rank, at * rows : (at + 1) * rows, :],
             sem.at[at - 2, rank],
         )
         for at, ref in ((2, v_ref), (3, g_ref))
@@ -53,20 +53,8 @@
     for at, copy in enumerate(whole_copies):
         copy.wait()
         for rank in range(ranks):
-            built_ref[rank, at * rows : (at + 1) * rows, :] = whole_ref[at, :, rank * width : (rank + 1) * width]
-    halves = [
-        pltpu.make_async_copy(
-            built_ref.at[:, half * rows : (half + 2) * rows, :],
-            out_ref.at[:, half * rows : (half + 2) * rows, :],
-            out_sem.at[half // 2],
-        )
-        for half in (0, 2)
-    ]
-    halves[0].start()
+            out_ref[rank, at * rows : (at + 1) * rows, :] = whole_ref[at, :, rank * width : (rank + 1) * width]
     for copy in copies:
-        copy.wait()
-    halves[1].start()
-    for copy in halves:
         copy.wait()
 
 
@@ -203,15 +191,13 @@
 
     by_rank = pl.pallas_call(
         split_kernel,
-        out_shape=jax.ShapeDtypeStruct((ranks, 4 * rows, width), bf16),
+        out_shape=pltpu.VMEM((ranks, 4 * rows, width), bf16),
         in_specs=[in_place()] * 4,
-        out_specs=in_place(),
+        out_specs=whole(),
         scratch_shapes=[
             pltpu.VMEM((2, rows, feat), bf16),
-            pltpu.VMEM((ranks, 4 * rows, width), bf16),
             pltpu.SemaphoreType.DMA((2,)),
             pltpu.SemaphoreType.DMA((2, ranks)),
-            pltpu.SemaphoreType.DMA((2,)),
         ],
         compiler_params=PARAMS,
     )(*(from_hbm(array) for array in (queries, keys, values, out_grad)))

time: 86.4 us -> 86.4 us (level)
  no operation moved by 1% of the time
where the time goes in v4:
time: 86.4 us; the launch traced here: 86 us
  blocking collectives  57.6 us (67%)
  waiting for transfers between devices  10.8 us (12%)
  starting transfers between devices  10.3 us (12%)
  Pallas kernels  6.69 us (8%)
    all_to_all x1, blocking collectives, local(): lax.all_to_all(in_slots.reshape(groups, PATCH_MAX, 3 * width), 'dp', spli...  42 us
    all_to_all x1, blocking collectives, local(): lax.all_to_all(packed.reshape(ranks, rows, 3 * width), 'tensor', split_ax...  15.5 us
    all_to_all x1, waiting for transfers between devices, local(): lax.all_to_all(by_rank, 'tensor', split_axis=0, concat_axis=0, tiled=True)  10.8 us
    all_to_all x1, starting transfers between devices, local(): lax.all_to_all(by_rank, 'tensor', split_axis=0, concat_axis=0, tiled=True)  10.3 us
    pallas_call x1, Pallas kernels, local(): pl.pallas_call(split_kernel, out_shape=pltpu.VMEM((ranks, 4 * rows, width...  2.31 us
  transfers between devices with their start and end apart: 1, of which 1 were waited for; matrix products, arithmetic and copies ran while one was open for 0% of the time, Pallas kernels for 2%

profile of v4, /device:TPU:1, one launch (start us, length us, event | category | flops | bytes accessed | tf_op | source)
XLA Modules:
  0.0 86.0 jit_solution(17245631855374332755)
XLA Ops:
  0.6 2.3 %shard_map.103 = bf16[8,128,384]{2,1,0:T(8,128)(2,1)} custom-call(bf16[32,3072]{1,0:T(8,128)(2,1)} %q_ref.1, bf16[32,3072]{1,0:T(8,128)(2,1)} %k_ref.1, bf16[32,3072]{1,0:T(8,128)(2,1)} %v_ref.1, bf16[32,3072]{1,0:T(8,128)(2,1)} %g_ref.1), custom_call_target="tpu_custom_call" | custom-call | tf_op jit(solution)/shard_map/pallas_call | solution.py:192
  3.0 0.0 copy-start
  3.0 10.3 %all-to-all-start = ((bf16[8,128,384]{2,1,0:T(8,128)(2,1)}), bf16[8,128,384]{2,1,0:T(8,128)(2,1)S(1)}, u32[]{:S(2)}, u32[]{:S(2)}) async-start(bf16[8,128,384]{2,1,0:T(8,128)(2,1)} %shard_map.103), calls=%async_computation | async-start | bytes 1572864 | tf_op jit(solution)/shard_map/all_to_all | solution.py:205
  13.3 0.0 copy-done
  13.3 1.6 %shard_map.104 = (f32[256,256]{1,0:T(8,128)S(1)}, f32[256,128]{1,0:T(8,128)S(1)}, bf16[512,256]{1,0:T(8,128)(2,1)S(1)}, bf16[256,512]{1,0:T(8,128)(2,1)S(1)}) custom-call(s32[1]{0:T(128)} %bitcast.at_ref, s32[32,64]{1,0:T(8,128)} %bitcast.10, s32[32,64]{1,0:T(8,128)} %bitcast.11, s32[32,64]{1,0:T(8,128)} %bitcast.12, s32[8]{0:T(128)S(1)} %copy-done), custom_call_target="tpu_custom_call" | custom-call | flops 16777216 | bytes 1048576 | tf_op jit(solution)/shard_map/pallas_call | solution.py:206
  14.9 10.8 %all-to-all-done.x_ref = bf16[8,128,384]{2,1,0:T(8,128)(2,1)S(1)} async-done(((bf16[8,128,384]{2,1,0:T(8,128)(2,1)}), bf16[8,128,384]{2,1,0:T(8,128)(2,1)S(1)}, u32[]{:S(2)}, u32[]{:S(2)}) %all-to-all-start) | async-done | bytes 786464 | tf_op jit(solution)/shard_map/all_to_all | solution.py:205
  25.6 1.5 %shard_map.105 = bf16[512,1152]{1,0:T(8,128)(2,1)S(1)} custom-call(f32[256,256]{1,0:T(8,128)S(1)} %get-tuple-element.11.same_ref, f32[256,128]{1,0:T(8,128)S(1)} %get-tuple-element.12.scale_ref, bf16[512,256]{1,0:T(8,128)(2,1)S(1)} %get-tuple-element.13.place_ref, bf16[8,128,384]{2,1,0:T(8,128)(2,1)S(1)} %all-to-all-done.x_ref), custom_call_target="tpu_custom_call" | custom-call | tf_op jit(solution)/shard_map/pallas_call | solution.py:219
  27.1 42.0 %all_to_all.15 = bf16[64,8,1152]{2,1,0:T(8,128)(2,1)S(1)} all-to-all(bf16[64,8,1152]{2,1,0:T(8,128)(2,1)S(1)} %bitcast.7), channel_id=1, replica_groups={{0,216,432,136,352,56,272,488,192,408,112,328,32,248,464,168,384,88,304..., dimensions={0} | all-to-all | bytes 2359296 | tf_op jit(solution)/shard_map/all_to_all | solution.py:226
  69.1 0.5 shard_map.106
  69.6 15.5 %all_to_all.16.x_ref = bf16[8,32,1152]{2,1,0:T(8,128)(2,1)S(1)} all-to-all(bf16[8,32,1152]{2,1,0:T(8,128)(2,1)S(1)} %bitcast.9), channel_id=1, replica_groups=mesh['dp'=64,'tensor'=8] {'tensor'}, dimensions={0} | all-to-all | bytes 1179648 | tf_op jit(solution)/shard_map/all_to_all | solution.py:241
  85.2 0.8 shard_map.107
Async XLA Ops:
  3.0 10.4 %copy-start = (s32[8]{0:T(128)S(1)}, s32[8]{0:T(128)}, u32[]{:S(2)}) copy-start(s32[8]{0:T(128)} %weights_ref.1) | copy-start | bytes 100
  3.0 22.6 %all-to-all-start = ((bf16[8,128,384]{2,1,0:T(8,128)(2,1)}), bf16[8,128,384]{2,1,0:T(8,128)(2,1)S(1)}, u32[]{:S(2)}, u32[]{:S(2)}) async-start(bf16[8,128,384]{2,1,0:T(8,128)(2,1)} %shard_map.103), calls=%async_computation | async-start | bytes 1572864 | tf_op jit(solution)/shard_map/all_to_all | solution.py:205

commit v5 on v4

--- a/solution.py
+++ b/solution.py
@@ -33,29 +33,22 @@
     return mask.astype(jnp.float32).astype(jnp.bfloat16)
 
 
-def split_kernel(q_ref, k_ref, v_ref, g_ref, out_ref, whole_ref, whole_sem, sem):
-    ranks, _, width = out_ref.shape
-    rows = q_ref.shape[0]
-    whole_copies = [
-        pltpu.make_async_copy(ref, whole_ref.at[at], whole_sem.at[at]) for at, ref in enumerate((q_ref, k_ref))
+def split_kernel(q_ref, k_ref, v_ref, g_ref, out_ref, whole_ref, sem):
+    ranks = out_ref.shape[0]
+    rows, feat = q_ref.shape
+    heads = feat // HEAD_DIM // ranks
+    copies = [
+        pltpu.make_async_copy(ref, whole_ref.at[at], sem.at[at]) for at, ref in enumerate((q_ref, k_ref, v_ref, g_ref))
     ]
-    copies = [
-        pltpu.make_async_copy(
-            ref.at[:, rank * width : (rank + 1) * width],
-            out_ref.at[rank, at * rows : (at + 1) * rows, :],
-            sem.at[at - 2, rank],
-        )
-        for at, ref in ((2, v_ref), (3, g_ref))
-        for rank in range(ranks)
-    ]
-    for copy in whole_copies + copies:
+    for copy in copies:
         copy.start()
-    for at, copy in enumerate(whole_copies):
+    for at, copy in enumerate(copies):
         copy.wait()
         for rank in range(ranks):
-            out_ref[rank, at * rows : (at + 1) * rows, :] = whole_ref[at, :, rank * width : (rank + 1) * width]
-    for copy in copies:
-        copy.wait()
+            for head in range(heads):
+                to = (head * 4 + at) * rows
+                col = (rank * heads + head) * HEAD_DIM
+                out_ref[rank, to : to + rows, :] = whole_ref[at, :, col : col + HEAD_DIM]
 
 
 def spread_column(column):
@@ -112,16 +105,17 @@
 
 
 def grad_kernel(same_ref, scale_ref, place_ref, x_ref, out_ref):
-    ranks, four_rows, width = x_ref.shape
-    rows = four_rows // 4
-    total = ranks * rows
+    ranks = x_ref.shape[0]
+    total = same_ref.shape[0]
+    rows = total // ranks
+    width = out_ref.shape[1] // 3
     heads = range(width // HEAD_DIM)
     mask = same_ref[...]
     place = place_ref[...]
 
     def rows_of(at, head):
-        cols = slice(head * HEAD_DIM, (head + 1) * HEAD_DIM)
-        return x_ref[:, at * rows : (at + 1) * rows, cols].reshape(total, HEAD_DIM)
+        begin = (head * 4 + at) * rows
+        return x_ref[:, begin : begin + rows, :].reshape(total, HEAD_DIM)
 
     def send(at, product):
         out_ref[:, at * width : (at + 1) * width] = product.astype(jnp.bfloat16)
@@ -147,16 +141,23 @@
 
 
 def pack_kernel(place_ref, x_ref, out_ref):
-    out_ref[...] = dot(place_ref[...], x_ref[...], NN).astype(jnp.bfloat16)
+    ranks, three_rows, width = out_ref.shape
+    rows = three_rows // 3
+    packed = dot(place_ref[...], x_ref[...], NN).astype(jnp.bfloat16)
+    for rank in range(ranks):
+        for at in range(3):
+            out_ref[rank, at * rows : (at + 1) * rows, :] = packed[
+                rank * rows : (rank + 1) * rows, at * width : (at + 1) * width
+            ]
 
 
 def join_kernel(x_ref, q_ref, k_ref, v_ref, whole_ref, sem):
-    ranks, _, wide = x_ref.shape
-    width = wide // 3
+    ranks, three_rows, width = x_ref.shape
+    rows = three_rows // 3
     copies = []
     for at, ref in enumerate((q_ref, k_ref, v_ref)):
         for rank in range(ranks):
-            whole_ref[at, :, rank * width : (rank + 1) * width] = x_ref[rank, :, at * width : (at + 1) * width]
+            whole_ref[at, :, rank * width : (rank + 1) * width] = x_ref[rank, at * rows : (at + 1) * rows, :]
         copies.append(pltpu.make_async_copy(whole_ref.at[at], ref, sem.at[at]))
         copies[-1].start()
     for copy in copies:
@@ -191,14 +192,10 @@
 
     by_rank = pl.pallas_call(
         split_kernel,
-        out_shape=pltpu.VMEM((ranks, 4 * rows, width), bf16),
+        out_shape=jax.ShapeDtypeStruct((ranks, 4 * rows * (width // HEAD_DIM), HEAD_DIM), bf16),
         in_specs=[in_place()] * 4,
         out_specs=whole(),
-        scratch_shapes=[
-            pltpu.VMEM((2, rows, feat), bf16),
-            pltpu.SemaphoreType.DMA((2,)),
-            pltpu.SemaphoreType.DMA((2, ranks)),
-        ],
+        scratch_shapes=[pltpu.VMEM((4, rows, feat), bf16), pltpu.SemaphoreType.DMA((4,))],
         compiler_params=PARAMS,
     )(*(from_hbm(array) for array in (queries, keys, values, out_grad)))
     by_rank, index = lax.optimization_barrier((by_rank, index))
@@ -233,14 +230,12 @@
     ).reshape(slots, 3 * width)
     packed = pl.pallas_call(
         pack_kernel,
-        out_shape=jax.ShapeDtypeStruct((total, 3 * width), bf16),
+        out_shape=jax.ShapeDtypeStruct((ranks, 3 * rows, width), bf16),
         in_specs=[whole()] * 2,
         out_specs=whole(),
         compiler_params=PARAMS,
     )(in_place_hot, arrived)
-    returned = lax.all_to_all(
-        packed.reshape(ranks, rows, 3 * width), "tensor", split_axis=0, concat_axis=0, tiled=True
-    )
+    returned = lax.all_to_all(packed, "tensor", split_axis=0, concat_axis=0, tiled=True)
     out = jax.ShapeDtypeStruct((rows, feat), bf16)
     return pl.pallas_call(
         join_kernel,

time: 86.4 us -> 86.3 us (level)
  no operation moved by 1% of the time
where the time goes in v5:
time: 86.3 us; the launch traced here: 85.9 us
  blocking collectives  57.6 us (67%)
  waiting for transfers between devices  10.8 us (13%)
  starting transfers between devices  10.3 us (12%)
  Pallas kernels  6.55 us (8%)
    all_to_all x1, blocking collectives, local(): lax.all_to_all(in_slots.reshape(groups, PATCH_MAX, 3 * width), 'dp', spli...  42 us
    all_to_all x1, blocking collectives, local(): lax.all_to_all(packed, 'tensor', split_axis=0, concat_axis=0, tiled=True)  15.6 us
    all_to_all x1, waiting for transfers between devices, local(): lax.all_to_all(by_rank, 'tensor', split_axis=0, concat_axis=0, tiled=True)  10.8 us
    all_to_all x1, starting transfers between devices, local(): lax.all_to_all(by_rank, 'tensor', split_axis=0, concat_axis=0, tiled=True)  10.3 us
    pallas_call x1, Pallas kernels, local(): pl.pallas_call(split_kernel, out_shape=jax.ShapeDtypeStruct((ranks, 4 * r...  2.18 us
  transfers between devices with their start and end apart: 1, of which 1 were waited for; matrix products, arithmetic and copies ran while one was open for 0% of the time, Pallas kernels for 2%

profile of v5, /device:TPU:1, one launch (start us, length us, event | category | flops | bytes accessed | tf_op | source)
XLA Modules:
  0.0 85.9 jit_solution(7157928784011799681)
XLA Ops:
  0.6 2.2 %shard_map.103 = bf16[8,384,128]{2,1,0:T(8,128)(2,1)} custom-call(bf16[32,3072]{1,0:T(8,128)(2,1)} %q_ref.1, bf16[32,3072]{1,0:T(8,128)(2,1)} %k_ref.1, bf16[32,3072]{1,0:T(8,128)(2,1)} %v_ref.1, bf16[32,3072]{1,0:T(8,128)(2,1)} %g_ref.1), custom_call_target="tpu_custom_call" | custom-call | tf_op jit(solution)/shard_map/pallas_call | solution.py:193
  2.8 0.0 copy-start
  2.8 10.3 %all-to-all-start = ((bf16[8,384,128]{2,1,0:T(8,128)(2,1)}), bf16[8,384,128]{2,1,0:T(8,128)(2,1)S(1)}, u32[]{:S(2)}, u32[]{:S(2)}) async-start(bf16[8,384,128]{2,1,0:T(8,128)(2,1)} %shard_map.103), calls=%async_computation | async-start | bytes 1572864 | tf_op jit(solution)/shard_map/all_to_all | solution.py:202
  13.2 0.0 copy-done
  13.2 1.5 %shard_map.104 = (f32[256,256]{1,0:T(8,128)S(1)}, f32[256,128]{1,0:T(8,128)S(1)}, bf16[512,256]{1,0:T(8,128)(2,1)S(1)}, bf16[256,512]{1,0:T(8,128)(2,1)S(1)}) custom-call(s32[1]{0:T(128)} %bitcast.at_ref, s32[32,64]{1,0:T(8,128)} %bitcast.8, s32[32,64]{1,0:T(8,128)} %bitcast.9, s32[32,64]{1,0:T(8,128)} %bitcast.10, s32[8]{0:T(128)S(1)} %copy-done), custom_call_target="tpu_custom_call" | custom-call | flops 16777216 | bytes 1048576 | tf_op jit(solution)/shard_map/pallas_call | solution.py:203
  14.7 10.8 %all-to-all-done.x_ref = bf16[8,384,128]{2,1,0:T(8,128)(2,1)S(1)} async-done(((bf16[8,384,128]{2,1,0:T(8,128)(2,1)}), bf16[8,384,128]{2,1,0:T(8,128)(2,1)S(1)}, u32[]{:S(2)}, u32[]{:S(2)}) %all-to-all-start) | async-done | bytes 786464 | tf_op jit(solution)/shard_map/all_to_all | solution.py:202
  25.5 1.5 %shard_map.105 = bf16[512,1152]{1,0:T(8,128)(2,1)S(1)} custom-call(f32[256,256]{1,0:T(8,128)S(1)} %get-tuple-element.11.same_ref, f32[256,128]{1,0:T(8,128)S(1)} %get-tuple-element.12.scale_ref, bf16[512,256]{1,0:T(8,128)(2,1)S(1)} %get-tuple-element.13.place_ref, bf16[8,384,128]{2,1,0:T(8,128)(2,1)S(1)} %all-to-all-done.x_ref), custom_call_target="tpu_custom_call" | custom-call | tf_op jit(solution)/shard_map/pallas_call | solution.py:216
  27.0 42.0 %all_to_all.15 = bf16[64,8,1152]{2,1,0:T(8,128)(2,1)S(1)} all-to-all(bf16[64,8,1152]{2,1,0:T(8,128)(2,1)S(1)} %bitcast.6), channel_id=1, replica_groups={{0,216,432,136,352,56,272,488,192,408,112,328,32,248,464,168,384,88,304..., dimensions={0} | all-to-all | bytes 2359296 | tf_op jit(solution)/shard_map/all_to_all | solution.py:223
  69.0 0.5 shard_map.106
  69.5 15.6 %all_to_all.16.x_ref = bf16[8,96,384]{2,1,0:T(8,128)(2,1)S(1)} all-to-all(bf16[8,96,384]{2,1,0:T(8,128)(2,1)S(1)} %shard_map.106), channel_id=1, replica_groups=mesh['dp'=64,'tensor'=8] {'tensor'}, dimensions={0} | all-to-all | bytes 1179648 | tf_op jit(solution)/shard_map/all_to_all | solution.py:238
  85.0 0.8 shard_map.107
Async XLA Ops:
  2.8 10.4 %copy-start = (s32[8]{0:T(128)S(1)}, s32[8]{0:T(128)}, u32[]{:S(2)}) copy-start(s32[8]{0:T(128)} %weights_ref.1) | copy-start | bytes 100
  2.8 22.6 %all-to-all-start = ((bf16[8,384,128]{2,1,0:T(8,128)(2,1)}), bf16[8,384,128]{2,1,0:T(8,128)(2,1)S(1)}, u32[]{:S(2)}, u32[]{:S(2)}) async-start(bf16[8,384,128]{2,1,0:T(8,128)(2,1)} %shard_map.103), calls=%async_computation | async-start | bytes 1572864 | tf_op jit(solution)/shard_map/all_to_all | solution.py:202

commit v6 on v5

--- a/solution.py
+++ b/solution.py
@@ -33,22 +33,35 @@
     return mask.astype(jnp.float32).astype(jnp.bfloat16)
 
 
-def split_kernel(q_ref, k_ref, v_ref, g_ref, out_ref, whole_ref, sem):
+def split_kernel(q_ref, k_ref, v_ref, g_ref, out_ref, whole_ref, built_ref, sem, out_sem):
     ranks = out_ref.shape[0]
     rows, feat = q_ref.shape
     heads = feat // HEAD_DIM // ranks
+    half = rows // 2
     copies = [
-        pltpu.make_async_copy(ref, whole_ref.at[at], sem.at[at]) for at, ref in enumerate((q_ref, k_ref, v_ref, g_ref))
+        pltpu.make_async_copy(
+            ref.at[part * half : (part + 1) * half, :],
+            whole_ref.at[at, part * half : (part + 1) * half, :],
+            sem.at[at, part],
+        )
+        for at, ref in enumerate((q_ref, k_ref, v_ref, g_ref))
+        for part in range(2)
     ]
     for copy in copies:
         copy.start()
-    for at, copy in enumerate(copies):
+    for copy in copies:
         copy.wait()
-        for rank in range(ranks):
-            for head in range(heads):
+    sends = []
+    for rank in range(ranks):
+        for head in range(heads):
+            for at in range(4):
                 to = (head * 4 + at) * rows
                 col = (rank * heads + head) * HEAD_DIM
-                out_ref[rank, to : to + rows, :] = whole_ref[at, :, col : col + HEAD_DIM]
+                built_ref[rank, to : to + rows, :] = whole_ref[at, :, col : col + HEAD_DIM]
+        sends.append(pltpu.make_async_copy(built_ref.at[rank], out_ref.at[rank], out_sem.at[rank]))
+        sends[-1].start()
+    for send in sends:
+        send.wait()
 
 
 def spread_column(column):
@@ -154,12 +167,16 @@
 def join_kernel(x_ref, q_ref, k_ref, v_ref, whole_ref, sem):
     ranks, three_rows, width = x_ref.shape
     rows = three_rows // 3
+    half = rows // 2
     copies = []
     for at, ref in enumerate((q_ref, k_ref, v_ref)):
-        for rank in range(ranks):
-            whole_ref[at, :, rank * width : (rank + 1) * width] = x_ref[rank, at * rows : (at + 1) * rows, :]
-        copies.append(pltpu.make_async_copy(whole_ref.at[at], ref, sem.at[at]))
-        copies[-1].start()
+        for part in range(2):
+            here = slice(part * half, (part + 1) * half)
+            begin = at * rows + part * half
+            for rank in range(ranks):
+                whole_ref[at, here, rank * width : (rank + 1) * width] = x_ref[rank, begin : begin + half, :]
+            copies.append(pltpu.make_async_copy(whole_ref.at[at, here, :], ref.at[here, :], sem.at[at, part]))
+            copies[-1].start()
     for copy in copies:
         copy.wait()
 
@@ -194,8 +211,13 @@
         split_kernel,
         out_shape=jax.ShapeDtypeStruct((ranks, 4 * rows * (width // HEAD_DIM), HEAD_DIM), bf16),
         in_specs=[in_place()] * 4,
-        out_specs=whole(),
-        scratch_shapes=[pltpu.VMEM((4, rows, feat), bf16), pltpu.SemaphoreType.DMA((4,))],
+        out_specs=in_place(),
+        scratch_shapes=[
+            pltpu.VMEM((4, rows, feat), bf16),
+            pltpu.VMEM((ranks, 4 * rows * (width // HEAD_DIM), HEAD_DIM), bf16),
+            pltpu.SemaphoreType.DMA((4, 2)),
+            pltpu.SemaphoreType.DMA((ranks,)),
+        ],
         compiler_params=PARAMS,
     )(*(from_hbm(array) for array in (queries, keys, values, out_grad)))
     by_rank, index = lax.optimization_barrier((by_rank, index))
@@ -242,7 +264,7 @@
         out_shape=(out, out, out),
         in_specs=[whole()],
         out_specs=(in_place(), in_place(), in_place()),
-        scratch_shapes=[pltpu.VMEM((3, rows, feat), bf16), pltpu.SemaphoreType.DMA((3,))],
+        scratch_shapes=[pltpu.VMEM((3, rows, feat), bf16), pltpu.SemaphoreType.DMA((3, 2))],
         compiler_params=PARAMS,
     )(returned)
 

time: 86.3 us -> 86.4 us (level)
  no operation moved by 1% of the time
where the time goes in v6:
time: 86.4 us; the launch traced here: 86 us
  blocking collectives  57.6 us (67%)
  waiting for transfers between devices  10.8 us (12%)
  starting transfers between devices  10.3 us (12%)
  Pallas kernels  6.65 us (8%)
    all_to_all x1, blocking collectives, local(): lax.all_to_all(in_slots.reshape(groups, PATCH_MAX, 3 * width), 'dp', spli...  42 us
    all_to_all x1, blocking collectives, local(): lax.all_to_all(packed, 'tensor', split_axis=0, concat_axis=0, tiled=True)  15.6 us
    all_to_all x1, waiting for transfers between devices, local(): lax.all_to_all(by_rank, 'tensor', split_axis=0, concat_axis=0, tiled=True)  10.8 us
    all_to_all x1, starting transfers between devices, local(): lax.all_to_all(by_rank, 'tensor', split_axis=0, concat_axis=0, tiled=True)  10.3 us
    pallas_call x1, Pallas kernels, local(): pl.pallas_call(split_kernel, out_shape=jax.ShapeDtypeStruct((ranks, 4 * r...  2.26 us
  transfers between devices with their start and end apart: 1, of which 1 were waited for; matrix products, arithmetic and copies ran while one was open for 0% of the time, Pallas kernels for 2%

profile of v6, /device:TPU:1, one launch (start us, length us, event | category | flops | bytes accessed | tf_op | source)
XLA Modules:
  0.0 86.0 jit_solution(2832753716843115401)
XLA Ops:
  0.6 2.3 %shard_map.103 = bf16[8,384,128]{2,1,0:T(8,128)(2,1)} custom-call(bf16[32,3072]{1,0:T(8,128)(2,1)} %q_ref.1, bf16[32,3072]{1,0:T(8,128)(2,1)} %k_ref.1, bf16[32,3072]{1,0:T(8,128)(2,1)} %v_ref.1, bf16[32,3072]{1,0:T(8,128)(2,1)} %g_ref.1), custom_call_target="tpu_custom_call" | custom-call | tf_op jit(solution)/shard_map/pallas_call | solution.py:210
  2.9 0.0 copy-start
  2.9 10.3 %all-to-all-start = ((bf16[8,384,128]{2,1,0:T(8,128)(2,1)}), bf16[8,384,128]{2,1,0:T(8,128)(2,1)S(1)}, u32[]{:S(2)}, u32[]{:S(2)}) async-start(bf16[8,384,128]{2,1,0:T(8,128)(2,1)} %shard_map.103), calls=%async_computation | async-start | bytes 1572864 | tf_op jit(solution)/shard_map/all_to_all | solution.py:224
  13.3 0.0 copy-done
  13.3 1.5 %shard_map.104 = (f32[256,256]{1,0:T(8,128)S(1)}, f32[256,128]{1,0:T(8,128)S(1)}, bf16[512,256]{1,0:T(8,128)(2,1)S(1)}, bf16[256,512]{1,0:T(8,128)(2,1)S(1)}) custom-call(s32[1]{0:T(128)} %bitcast.at_ref, s32[32,64]{1,0:T(8,128)} %bitcast.8, s32[32,64]{1,0:T(8,128)} %bitcast.9, s32[32,64]{1,0:T(8,128)} %bitcast.10, s32[8]{0:T(128)S(1)} %copy-done), custom_call_target="tpu_custom_call" | custom-call | flops 16777216 | bytes 1048576 | tf_op jit(solution)/shard_map/pallas_call | solution.py:225
  14.8 10.8 %all-to-all-done.x_ref = bf16[8,384,128]{2,1,0:T(8,128)(2,1)S(1)} async-done(((bf16[8,384,128]{2,1,0:T(8,128)(2,1)}), bf16[8,384,128]{2,1,0:T(8,128)(2,1)S(1)}, u32[]{:S(2)}, u32[]{:S(2)}) %all-to-all-start) | async-done | bytes 786464 | tf_op jit(solution)/shard_map/all_to_all | solution.py:224
  25.6 1.5 %shard_map.105 = bf16[512,1152]{1,0:T(8,128)(2,1)S(1)} custom-call(f32[256,256]{1,0:T(8,128)S(1)} %get-tuple-element.11.same_ref, f32[256,128]{1,0:T(8,128)S(1)} %get-tuple-element.12.scale_ref, bf16[512,256]{1,0:T(8,128)(2,1)S(1)} %get-tuple-element.13.place_ref, bf16[8,384,128]{2,1,0:T(8,128)(2,1)S(1)} %all-to-all-done.x_ref), custom_call_target="tpu_custom_call" | custom-call | tf_op jit(solution)/shard_map/pallas_call | solution.py:238
  27.0 42.0 %all_to_all.15 = bf16[64,8,1152]{2,1,0:T(8,128)(2,1)S(1)} all-to-all(bf16[64,8,1152]{2,1,0:T(8,128)(2,1)S(1)} %bitcast.6), channel_id=1, replica_groups={{0,216,432,136,352,56,272,488,192,408,112,328,32,248,464,168,384,88,304..., dimensions={0} | all-to-all | bytes 2359296 | tf_op jit(solution)/shard_map/all_to_all | solution.py:245
  69.0 0.5 shard_map.106
  69.6 15.6 %all_to_all.16.x_ref = bf16[8,96,384]{2,1,0:T(8,128)(2,1)S(1)} all-to-all(bf16[8,96,384]{2,1,0:T(8,128)(2,1)S(1)} %shard_map.106), channel_id=1, replica_groups=mesh['dp'=64,'tensor'=8] {'tensor'}, dimensions={0} | all-to-all | bytes 1179648 | tf_op jit(solution)/shard_map/all_to_all | solution.py:260
  85.1 0.9 %shard_map.107 = (bf16[32,3072]{1,0:T(8,128)(2,1)}, bf16[32,3072]{1,0:T(8,128)(2,1)}, bf16[32,3072]{1,0:T(8,128)(2,1)}) custom-call(bf16[8,96,384]{2,1,0:T(8,128)(2,1)S(1)} %all_to_all.16.x_ref), custom_call_target="tpu_custom_call" | custom-call | tf_op jit(solution)/shard_map/pallas_call | solution.py:262
Async XLA Ops:
  2.9 10.4 %copy-start = (s32[8]{0:T(128)S(1)}, s32[8]{0:T(128)}, u32[]{:S(2)}) copy-start(s32[8]{0:T(128)} %weights_ref.1) | copy-start | bytes 100
  2.9 22.6 %all-to-all-start = ((bf16[8,384,128]{2,1,0:T(8,128)(2,1)}), bf16[8,384,128]{2,1,0:T(8,128)(2,1)S(1)}, u32[]{:S(2)}, u32[]{:S(2)}) async-start(bf16[8,384,128]{2,1,0:T(8,128)(2,1)} %shard_map.103), calls=%async_computation | async-start | bytes 1572864 | tf_op jit(solution)/shard_map/all_to_all | solution.py:224

commit v7 on v5

--- a/solution.py
+++ b/solution.py
@@ -15,8 +15,8 @@
 NT = (((1,), (1,)), ((), ()))
 TN = (((0,), (0,)), ((), ()))
 
-STRIDE = 27
-UNSTRIDE = 19
+STRIDE = 45
+UNSTRIDE = 37
 
 PARAMS = pltpu.CompilerParams(vmem_limit_bytes=48 * 1024 * 1024)
 

time: 86.3 us -> 84.7 us (0.981)
  blocking collectives: 57.6 us -> 55.9 us
    all_to_all x1, blocking collectives: 42 us -> 40.9 us  [local(): lax.all_to_all(in_slots.reshape(groups, PATCH_MAX, 3 * width), 'dp', spli...]
where the time goes in v7:
time: 84.7 us; the launch traced here: 84.2 us
  blocking collectives  55.9 us (66%)
  waiting for transfers between devices  10.8 us (13%)
  starting transfers between devices  10.3 us (12%)
  Pallas kernels  6.55 us (8%)
    all_to_all x1, blocking collectives, local(): lax.all_to_all(in_slots.reshape(groups, PATCH_MAX, 3 * width), 'dp', spli...  40.9 us
    all_to_all x1, blocking collectives, local(): lax.all_to_all(packed, 'tensor', split_axis=0, concat_axis=0, tiled=True)  14.9 us
    all_to_all x1, waiting for transfers between devices, local(): lax.all_to_all(by_rank, 'tensor', split_axis=0, concat_axis=0, tiled=True)  10.8 us
    all_to_all x1, starting transfers between devices, local(): lax.all_to_all(by_rank, 'tensor', split_axis=0, concat_axis=0, tiled=True)  10.3 us
    pallas_call x1, Pallas kernels, local(): pl.pallas_call(split_kernel, out_shape=jax.ShapeDtypeStruct((ranks, 4 * r...  2.18 us
  transfers between devices with their start and end apart: 1, of which 1 were waited for; matrix products, arithmetic and copies ran while one was open for 0% of the time, Pallas kernels for 2%

profile of v7, /device:TPU:1, one launch (start us, length us, event | category | flops | bytes accessed | tf_op | source)
XLA Modules:
  0.0 84.2 jit_solution(15518032745957397498)
XLA Ops:
  0.6 2.2 %shard_map.103 = bf16[8,384,128]{2,1,0:T(8,128)(2,1)} custom-call(bf16[32,3072]{1,0:T(8,128)(2,1)} %q_ref.1, bf16[32,3072]{1,0:T(8,128)(2,1)} %k_ref.1, bf16[32,3072]{1,0:T(8,128)(2,1)} %v_ref.1, bf16[32,3072]{1,0:T(8,128)(2,1)} %g_ref.1), custom_call_target="tpu_custom_call" | custom-call | tf_op jit(solution)/shard_map/pallas_call | solution.py:193
  2.8 0.0 copy-start
  2.8 10.3 %all-to-all-start = ((bf16[8,384,128]{2,1,0:T(8,128)(2,1)}), bf16[8,384,128]{2,1,0:T(8,128)(2,1)S(1)}, u32[]{:S(2)}, u32[]{:S(2)}) async-start(bf16[8,384,128]{2,1,0:T(8,128)(2,1)} %shard_map.103), calls=%async_computation | async-start | bytes 1572864 | tf_op jit(solution)/shard_map/all_to_all | solution.py:202
  13.2 0.0 copy-done
  13.2 1.5 %shard_map.104 = (f32[256,256]{1,0:T(8,128)S(1)}, f32[256,128]{1,0:T(8,128)S(1)}, bf16[512,256]{1,0:T(8,128)(2,1)S(1)}, bf16[256,512]{1,0:T(8,128)(2,1)S(1)}) custom-call(s32[1]{0:T(128)} %bitcast.at_ref, s32[32,64]{1,0:T(8,128)} %bitcast.8, s32[32,64]{1,0:T(8,128)} %bitcast.9, s32[32,64]{1,0:T(8,128)} %bitcast.10, s32[8]{0:T(128)S(1)} %copy-done), custom_call_target="tpu_custom_call" | custom-call | flops 16777216 | bytes 1048576 | tf_op jit(solution)/shard_map/pallas_call | solution.py:203
  14.7 10.8 %all-to-all-done.x_ref = bf16[8,384,128]{2,1,0:T(8,128)(2,1)S(1)} async-done(((bf16[8,384,128]{2,1,0:T(8,128)(2,1)}), bf16[8,384,128]{2,1,0:T(8,128)(2,1)S(1)}, u32[]{:S(2)}, u32[]{:S(2)}) %all-to-all-start) | async-done | bytes 786464 | tf_op jit(solution)/shard_map/all_to_all | solution.py:202
  25.5 1.5 %shard_map.105 = bf16[512,1152]{1,0:T(8,128)(2,1)S(1)} custom-call(f32[256,256]{1,0:T(8,128)S(1)} %get-tuple-element.11.same_ref, f32[256,128]{1,0:T(8,128)S(1)} %get-tuple-element.12.scale_ref, bf16[512,256]{1,0:T(8,128)(2,1)S(1)} %get-tuple-element.13.place_ref, bf16[8,384,128]{2,1,0:T(8,128)(2,1)S(1)} %all-to-all-done.x_ref), custom_call_target="tpu_custom_call" | custom-call | tf_op jit(solution)/shard_map/pallas_call | solution.py:216
  27.0 40.9 %all_to_all.15 = bf16[64,8,1152]{2,1,0:T(8,128)(2,1)S(1)} all-to-all(bf16[64,8,1152]{2,1,0:T(8,128)(2,1)S(1)} %bitcast.6), channel_id=1, replica_groups={{0,360,208,56,416,264,112,472,320,168,16,376,224,72,432,280,128,488,336..., dimensions={0} | all-to-all | bytes 2359296 | tf_op jit(solution)/shard_map/all_to_all | solution.py:223
  67.9 0.5 shard_map.106
  68.4 14.9 %all_to_all.16.x_ref = bf16[8,96,384]{2,1,0:T(8,128)(2,1)S(1)} all-to-all(bf16[8,96,384]{2,1,0:T(8,128)(2,1)S(1)} %shard_map.106), channel_id=1, replica_groups=mesh['dp'=64,'tensor'=8] {'tensor'}, dimensions={0} | all-to-all | bytes 1179648 | tf_op jit(solution)/shard_map/all_to_all | solution.py:238
  83.3 0.8 %shard_map.107 = (bf16[32,3072]{1,0:T(8,128)(2,1)}, bf16[32,3072]{1,0:T(8,128)(2,1)}, bf16[32,3072]{1,0:T(8,128)(2,1)}) custom-call(bf16[8,96,384]{2,1,0:T(8,128)(2,1)S(1)} %all_to_all.16.x_ref), custom_call_target="tpu_custom_call" | custom-call | tf_op jit(solution)/shard_map/pallas_call | solution.py:240
Async XLA Ops:
  2.8 10.4 %copy-start = (s32[8]{0:T(128)S(1)}, s32[8]{0:T(128)}, u32[]{:S(2)}) copy-start(s32[8]{0:T(128)} %weights_ref.1) | copy-start | bytes 100
  2.8 22.6 %all-to-all-start = ((bf16[8,384,128]{2,1,0:T(8,128)(2,1)}), bf16[8,384,128]{2,1,0:T(8,128)(2,1)S(1)}, u32[]{:S(2)}, u32[]{:S(2)}) async-start(bf16[8,384,128]{2,1,0:T(8,128)(2,1)} %shard_map.103), calls=%async_computation | async-start | bytes 1572864 | tf_op jit(solution)/shard_map/all_to_all | solution.py:202

commit v8 on v7

--- a/solution.py
+++ b/solution.py
@@ -15,8 +15,8 @@
 NT = (((1,), (1,)), ((), ()))
 TN = (((0,), (0,)), ((), ()))
 
-STRIDE = 45
-UNSTRIDE = 37
+STRIDE = 29
+UNSTRIDE = 53
 
 PARAMS = pltpu.CompilerParams(vmem_limit_bytes=48 * 1024 * 1024)
 

time: 84.7 us -> 84.8 us (level)
  no operation moved by 1% of the time
where the time goes in v8:
time: 84.8 us; the launch traced here: 84.4 us
  blocking collectives  56.1 us (66%)
  waiting for transfers between devices  10.8 us (13%)
  starting transfers between devices  10.3 us (12%)
  Pallas kernels  6.55 us (8%)
    all_to_all x1, blocking collectives, local(): lax.all_to_all(in_slots.reshape(groups, PATCH_MAX, 3 * width), 'dp', spli...  40.7 us
    all_to_all x1, blocking collectives, local(): lax.all_to_all(packed, 'tensor', split_axis=0, concat_axis=0, tiled=True)  15.4 us
    all_to_all x1, waiting for transfers between devices, local(): lax.all_to_all(by_rank, 'tensor', split_axis=0, concat_axis=0, tiled=True)  10.8 us
    all_to_all x1, starting transfers between devices, local(): lax.all_to_all(by_rank, 'tensor', split_axis=0, concat_axis=0, tiled=True)  10.3 us
    pallas_call x1, Pallas kernels, local(): pl.pallas_call(split_kernel, out_shape=jax.ShapeDtypeStruct((ranks, 4 * r...  2.18 us
  transfers between devices with their start and end apart: 1, of which 1 were waited for; matrix products, arithmetic and copies ran while one was open for 0% of the time, Pallas kernels for 2%

profile of v8, /device:TPU:1, one launch (start us, length us, event | category | flops | bytes accessed | tf_op | source)
XLA Modules:
  0.0 84.4 jit_solution(5122952647376313585)
XLA Ops:
  0.6 2.2 %shard_map.103 = bf16[8,384,128]{2,1,0:T(8,128)(2,1)} custom-call(bf16[32,3072]{1,0:T(8,128)(2,1)} %q_ref.1, bf16[32,3072]{1,0:T(8,128)(2,1)} %k_ref.1, bf16[32,3072]{1,0:T(8,128)(2,1)} %v_ref.1, bf16[32,3072]{1,0:T(8,128)(2,1)} %g_ref.1), custom_call_target="tpu_custom_call" | custom-call | tf_op jit(solution)/shard_map/pallas_call | solution.py:193
  2.8 0.0 copy-start
  2.8 10.3 %all-to-all-start = ((bf16[8,384,128]{2,1,0:T(8,128)(2,1)}), bf16[8,384,128]{2,1,0:T(8,128)(2,1)S(1)}, u32[]{:S(2)}, u32[]{:S(2)}) async-start(bf16[8,384,128]{2,1,0:T(8,128)(2,1)} %shard_map.103), calls=%async_computation | async-start | bytes 1572864 | tf_op jit(solution)/shard_map/all_to_all | solution.py:202
  13.2 0.0 copy-done
  13.2 1.5 %shard_map.104 = (f32[256,256]{1,0:T(8,128)S(1)}, f32[256,128]{1,0:T(8,128)S(1)}, bf16[512,256]{1,0:T(8,128)(2,1)S(1)}, bf16[256,512]{1,0:T(8,128)(2,1)S(1)}) custom-call(s32[1]{0:T(128)} %bitcast.at_ref, s32[32,64]{1,0:T(8,128)} %bitcast.8, s32[32,64]{1,0:T(8,128)} %bitcast.9, s32[32,64]{1,0:T(8,128)} %bitcast.10, s32[8]{0:T(128)S(1)} %copy-done), custom_call_target="tpu_custom_call" | custom-call | flops 16777216 | bytes 1048576 | tf_op jit(solution)/shard_map/pallas_call | solution.py:203
  14.7 10.8 %all-to-all-done.x_ref = bf16[8,384,128]{2,1,0:T(8,128)(2,1)S(1)} async-done(((bf16[8,384,128]{2,1,0:T(8,128)(2,1)}), bf16[8,384,128]{2,1,0:T(8,128)(2,1)S(1)}, u32[]{:S(2)}, u32[]{:S(2)}) %all-to-all-start) | async-done | bytes 786464 | tf_op jit(solution)/shard_map/all_to_all | solution.py:202
  25.5 1.5 %shard_map.105 = bf16[512,1152]{1,0:T(8,128)(2,1)S(1)} custom-call(f32[256,256]{1,0:T(8,128)S(1)} %get-tuple-element.11.same_ref, f32[256,128]{1,0:T(8,128)S(1)} %get-tuple-element.12.scale_ref, bf16[512,256]{1,0:T(8,128)(2,1)S(1)} %get-tuple-element.13.place_ref, bf16[8,384,128]{2,1,0:T(8,128)(2,1)S(1)} %all-to-all-done.x_ref), custom_call_target="tpu_custom_call" | custom-call | tf_op jit(solution)/shard_map/pallas_call | solution.py:216
  27.0 40.7 %all_to_all.15 = bf16[64,8,1152]{2,1,0:T(8,128)(2,1)S(1)} all-to-all(bf16[64,8,1152]{2,1,0:T(8,128)(2,1)S(1)} %bitcast.6), channel_id=1, replica_groups={{0,232,464,184,416,136,368,88,320,40,272,504,224,456,176,408,128,360,80..., dimensions={0} | all-to-all | bytes 2359296 | tf_op jit(solution)/shard_map/all_to_all | solution.py:223
  67.7 0.5 shard_map.106
  68.2 15.4 %all_to_all.16.x_ref = bf16[8,96,384]{2,1,0:T(8,128)(2,1)S(1)} all-to-all(bf16[8,96,384]{2,1,0:T(8,128)(2,1)S(1)} %shard_map.106), channel_id=1, replica_groups=mesh['dp'=64,'tensor'=8] {'tensor'}, dimensions={0} | all-to-all | bytes 1179648 | tf_op jit(solution)/shard_map/all_to_all | solution.py:238
  83.6 0.8 %shard_map.107 = (bf16[32,3072]{1,0:T(8,128)(2,1)}, bf16[32,3072]{1,0:T(8,128)(2,1)}, bf16[32,3072]{1,0:T(8,128)(2,1)}) custom-call(bf16[8,96,384]{2,1,0:T(8,128)(2,1)S(1)} %all_to_all.16.x_ref), custom_call_target="tpu_custom_call" | custom-call | tf_op jit(solution)/shard_map/pallas_call | solution.py:240
Async XLA Ops:
  2.8 10.4 %copy-start = (s32[8]{0:T(128)S(1)}, s32[8]{0:T(128)}, u32[]{:S(2)}) copy-start(s32[8]{0:T(128)} %weights_ref.1) | copy-start | bytes 100
  2.8 22.6 %all-to-all-start = ((bf16[8,384,128]{2,1,0:T(8,128)(2,1)}), bf16[8,384,128]{2,1,0:T(8,128)(2,1)S(1)}, u32[]{:S(2)}, u32[]{:S(2)}) async-start(bf16[8,384,128]{2,1,0:T(8,128)(2,1)} %shard_map.103), calls=%async_computation | async-start | bytes 1572864 | tf_op jit(solution)/shard_map/all_to_all | solution.py:202

commit v9 on v8

--- a/solution.py
+++ b/solution.py
@@ -15,6 +15,7 @@
 NT = (((1,), (1,)), ((), ()))
 TN = (((0,), (0,)), ((), ()))
 
+LINE = 8
 STRIDE = 29
 UNSTRIDE = 53
 
@@ -31,6 +32,10 @@
 
 def low(mask):
     return mask.astype(jnp.float32).astype(jnp.bfloat16)
+
+
+def turned(index):
+    return index % LINE * LINE + index // LINE
 
 
 def split_kernel(q_ref, k_ref, v_ref, g_ref, out_ref, whole_ref, sem):
@@ -87,6 +92,8 @@
         weight = jnp.where(kind == at, weights_ref[at].astype(jnp.float32) * 0.25, weight)
     scale_ref[...] = dot(member_low, spread_column(weight), TN)
 
+    line = jnp.floor(pack * (1.0 / LINE))
+    pack = (pack - line * LINE) * LINE + line
     place = pack * UNSTRIDE - jnp.floor(pack * (UNSTRIDE / groups)) * groups
     slot = jnp.sum(jnp.where(member, place * PATCH_MAX + prior + offset + 1.0, 0.0), axis=0, keepdims=True)
     slot = slot.astype(jnp.int32) - 1
@@ -96,7 +103,7 @@
     incoming = jnp.broadcast_to(jnp.sum(arriving, axis=0, keepdims=True), (8, groups))
     before = low(iota((groups, groups), 0) < iota((groups, groups), 1))
     begins = dot(incoming.astype(jnp.bfloat16), before, NN)
-    to_slots = low((iota((groups, slots), 1) // PATCH_MAX * STRIDE) % groups == iota((groups, slots), 0))
+    to_slots = low(turned(iota((groups, slots), 1) // PATCH_MAX * STRIDE % groups) == iota((groups, slots), 0))
     begin_at = dot(begins.astype(jnp.bfloat16), to_slots, NN)[0:1]
     count_at = dot(incoming.astype(jnp.bfloat16), to_slots, NN)[0:1]
     within = (iota((1, slots), 1) % PATCH_MAX).astype(jnp.float32)
@@ -225,7 +232,7 @@
         "dp",
         split_axis=0,
         concat_axis=0,
-        axis_index_groups=[[place * STRIDE % groups for place in range(groups)]],
+        axis_index_groups=[[turned(place * STRIDE % groups) for place in range(groups)]],
         tiled=True,
     ).reshape(slots, 3 * width)
     packed = pl.pallas_call(

time: 84.8 us -> 84.9 us (level)
  no operation moved by 1% of the time
where the time goes in v9:
time: 84.9 us; the launch traced here: 84.5 us
  blocking collectives  56.2 us (66%)
  waiting for transfers between devices  10.7 us (13%)
  starting transfers between devices  10.3 us (12%)
  Pallas kernels  6.56 us (8%)
    all_to_all x1, blocking collectives, local(): lax.all_to_all(in_slots.reshape(groups, PATCH_MAX, 3 * width), 'dp', spli...  40.9 us
    all_to_all x1, blocking collectives, local(): lax.all_to_all(packed, 'tensor', split_axis=0, concat_axis=0, tiled=True)  15.4 us
    all_to_all x1, waiting for transfers between devices, local(): lax.all_to_all(by_rank, 'tensor', split_axis=0, concat_axis=0, tiled=True)  10.7 us
    all_to_all x1, starting transfers between devices, local(): lax.all_to_all(by_rank, 'tensor', split_axis=0, concat_axis=0, tiled=True)  10.3 us
    pallas_call x1, Pallas kernels, local(): pl.pallas_call(split_kernel, out_shape=jax.ShapeDtypeStruct((ranks, 4 * r...  2.18 us
  transfers between devices with their start and end apart: 1, of which 1 were waited for; matrix products, arithmetic and copies ran while one was open for 0% of the time, Pallas kernels for 2%

profile of v9, /device:TPU:1, one launch (start us, length us, event | category | flops | bytes accessed | tf_op | source)
XLA Modules:
  0.0 84.5 jit_solution(5294250479979604397)
XLA Ops:
  0.6 2.2 %shard_map.103 = bf16[8,384,128]{2,1,0:T(8,128)(2,1)} custom-call(bf16[32,3072]{1,0:T(8,128)(2,1)} %q_ref.1, bf16[32,3072]{1,0:T(8,128)(2,1)} %k_ref.1, bf16[32,3072]{1,0:T(8,128)(2,1)} %v_ref.1, bf16[32,3072]{1,0:T(8,128)(2,1)} %g_ref.1), custom_call_target="tpu_custom_call" | custom-call | tf_op jit(solution)/shard_map/pallas_call | solution.py:200
  2.8 0.0 copy-start
  2.8 10.3 %all-to-all-start = ((bf16[8,384,128]{2,1,0:T(8,128)(2,1)}), bf16[8,384,128]{2,1,0:T(8,128)(2,1)S(1)}, u32[]{:S(2)}, u32[]{:S(2)}) async-start(bf16[8,384,128]{2,1,0:T(8,128)(2,1)} %shard_map.103), calls=%async_computation | async-start | bytes 1572864 | tf_op jit(solution)/shard_map/all_to_all | solution.py:209
  13.2 0.0 copy-done
  13.2 1.6 %shard_map.104 = (f32[256,256]{1,0:T(8,128)S(1)}, f32[256,128]{1,0:T(8,128)S(1)}, bf16[512,256]{1,0:T(8,128)(2,1)S(1)}, bf16[256,512]{1,0:T(8,128)(2,1)S(1)}) custom-call(s32[1]{0:T(128)} %bitcast.at_ref, s32[32,64]{1,0:T(8,128)} %bitcast.8, s32[32,64]{1,0:T(8,128)} %bitcast.9, s32[32,64]{1,0:T(8,128)} %bitcast.10, s32[8]{0:T(128)S(1)} %copy-done), custom_call_target="tpu_custom_call" | custom-call | flops 16777216 | bytes 1048576 | tf_op jit(solution)/shard_map/pallas_call | solution.py:210
  14.7 10.7 %all-to-all-done.x_ref = bf16[8,384,128]{2,1,0:T(8,128)(2,1)S(1)} async-done(((bf16[8,384,128]{2,1,0:T(8,128)(2,1)}), bf16[8,384,128]{2,1,0:T(8,128)(2,1)S(1)}, u32[]{:S(2)}, u32[]{:S(2)}) %all-to-all-start) | async-done | bytes 786464 | tf_op jit(solution)/shard_map/all_to_all | solution.py:209
  25.5 1.5 %shard_map.105 = bf16[512,1152]{1,0:T(8,128)(2,1)S(1)} custom-call(f32[256,256]{1,0:T(8,128)S(1)} %get-tuple-element.11.same_ref, f32[256,128]{1,0:T(8,128)S(1)} %get-tuple-element.12.scale_ref, bf16[512,256]{1,0:T(8,128)(2,1)S(1)} %get-tuple-element.13.place_ref, bf16[8,384,128]{2,1,0:T(8,128)(2,1)S(1)} %all-to-all-done.x_ref), custom_call_target="tpu_custom_call" | custom-call | tf_op jit(solution)/shard_map/pallas_call | solution.py:223
  27.0 40.9 %all_to_all.15 = bf16[64,8,1152]{2,1,0:T(8,128)(2,1)S(1)} all-to-all(bf16[64,8,1152]{2,1,0:T(8,128)(2,1)S(1)} %bitcast.6), channel_id=1, replica_groups={{0,344,184,464,304,80,424,200,40,320,160,504,280,120,400,240,16,360,136..., dimensions={0} | all-to-all | bytes 2359296 | tf_op jit(solution)/shard_map/all_to_all | solution.py:230
  67.8 0.5 shard_map.106
  68.3 15.4 %all_to_all.16.x_ref = bf16[8,96,384]{2,1,0:T(8,128)(2,1)S(1)} all-to-all(bf16[8,96,384]{2,1,0:T(8,128)(2,1)S(1)} %shard_map.106), channel_id=1, replica_groups=mesh['dp'=64,'tensor'=8] {'tensor'}, dimensions={0} | all-to-all | bytes 1179648 | tf_op jit(solution)/shard_map/all_to_all | solution.py:245
  83.7 0.8 %shard_map.107 = (bf16[32,3072]{1,0:T(8,128)(2,1)}, bf16[32,3072]{1,0:T(8,128)(2,1)}, bf16[32,3072]{1,0:T(8,128)(2,1)}) custom-call(bf16[8,96,384]{2,1,0:T(8,128)(2,1)S(1)} %all_to_all.16.x_ref), custom_call_target="tpu_custom_call" | custom-call | tf_op jit(solution)/shard_map/pallas_call | solution.py:247
Async XLA Ops:
  2.8 10.4 %copy-start = (s32[8]{0:T(128)S(1)}, s32[8]{0:T(128)}, u32[]{:S(2)}) copy-start(s32[8]{0:T(128)} %weights_ref.1) | copy-start | bytes 100
  2.8 22.6 %all-to-all-start = ((bf16[8,384,128]{2,1,0:T(8,128)(2,1)}), bf16[8,384,128]{2,1,0:T(8,128)(2,1)S(1)}, u32[]{:S(2)}, u32[]{:S(2)}) async-start(bf16[8,384,128]{2,1,0:T(8,128)(2,1)} %shard_map.103), calls=%async_computation | async-start | bytes 1572864 | tf_op jit(solution)/shard_map/all_to_all | solution.py:209

commit v10 on v9

--- a/solution.py
+++ b/solution.py
@@ -16,8 +16,8 @@
 TN = (((0,), (0,)), ((), ()))
 
 LINE = 8
-STRIDE = 29
-UNSTRIDE = 53
+STRIDE = 45
+UNSTRIDE = 37
 
 PARAMS = pltpu.CompilerParams(vmem_limit_bytes=48 * 1024 * 1024)
 

time: 84.9 us -> 85.2 us (level)
  no operation moved by 1% of the time
where the time goes in v10:
time: 85.2 us; the launch traced here: 84.8 us
  blocking collectives  56.5 us (66%)
  waiting for transfers between devices  10.7 us (13%)
  starting transfers between devices  10.3 us (12%)
  Pallas kernels  6.56 us (8%)
    all_to_all x1, blocking collectives, local(): lax.all_to_all(in_slots.reshape(groups, PATCH_MAX, 3 * width), 'dp', spli...  41.7 us
    all_to_all x1, blocking collectives, local(): lax.all_to_all(packed, 'tensor', split_axis=0, concat_axis=0, tiled=True)  14.9 us
    all_to_all x1, waiting for transfers between devices, local(): lax.all_to_all(by_rank, 'tensor', split_axis=0, concat_axis=0, tiled=True)  10.7 us
    all_to_all x1, starting transfers between devices, local(): lax.all_to_all(by_rank, 'tensor', split_axis=0, concat_axis=0, tiled=True)  10.3 us
    pallas_call x1, Pallas kernels, local(): pl.pallas_call(split_kernel, out_shape=jax.ShapeDtypeStruct((ranks, 4 * r...  2.18 us
  transfers between devices with their start and end apart: 1, of which 1 were waited for; matrix products, arithmetic and copies ran while one was open for 0% of the time, Pallas kernels for 2%

profile of v10, /device:TPU:1, one launch (start us, length us, event | category | flops | bytes accessed | tf_op | source)
XLA Modules:
  0.0 84.8 jit_solution(17943383277516205026)
XLA Ops:
  0.6 2.2 %shard_map.103 = bf16[8,384,128]{2,1,0:T(8,128)(2,1)} custom-call(bf16[32,3072]{1,0:T(8,128)(2,1)} %q_ref.1, bf16[32,3072]{1,0:T(8,128)(2,1)} %k_ref.1, bf16[32,3072]{1,0:T(8,128)(2,1)} %v_ref.1, bf16[32,3072]{1,0:T(8,128)(2,1)} %g_ref.1), custom_call_target="tpu_custom_call" | custom-call | tf_op jit(solution)/shard_map/pallas_call | solution.py:200
  2.8 0.0 copy-start
  2.8 10.3 %all-to-all-start = ((bf16[8,384,128]{2,1,0:T(8,128)(2,1)}), bf16[8,384,128]{2,1,0:T(8,128)(2,1)S(1)}, u32[]{:S(2)}, u32[]{:S(2)}) async-start(bf16[8,384,128]{2,1,0:T(8,128)(2,1)} %shard_map.103), calls=%async_computation | async-start | bytes 1572864 | tf_op jit(solution)/shard_map/all_to_all | solution.py:209
  13.2 0.0 copy-done
  13.2 1.6 %shard_map.104 = (f32[256,256]{1,0:T(8,128)S(1)}, f32[256,128]{1,0:T(8,128)S(1)}, bf16[512,256]{1,0:T(8,128)(2,1)S(1)}, bf16[256,512]{1,0:T(8,128)(2,1)S(1)}) custom-call(s32[1]{0:T(128)} %bitcast.at_ref, s32[32,64]{1,0:T(8,128)} %bitcast.8, s32[32,64]{1,0:T(8,128)} %bitcast.9, s32[32,64]{1,0:T(8,128)} %bitcast.10, s32[8]{0:T(128)S(1)} %copy-done), custom_call_target="tpu_custom_call" | custom-call | flops 16777216 | bytes 1048576 | tf_op jit(solution)/shard_map/pallas_call | solution.py:210
  14.7 10.7 %all-to-all-done.x_ref = bf16[8,384,128]{2,1,0:T(8,128)(2,1)S(1)} async-done(((bf16[8,384,128]{2,1,0:T(8,128)(2,1)}), bf16[8,384,128]{2,1,0:T(8,128)(2,1)S(1)}, u32[]{:S(2)}, u32[]{:S(2)}) %all-to-all-start) | async-done | bytes 786464 | tf_op jit(solution)/shard_map/all_to_all | solution.py:209
  25.5 1.5 %shard_map.105 = bf16[512,1152]{1,0:T(8,128)(2,1)S(1)} custom-call(f32[256,256]{1,0:T(8,128)S(1)} %get-tuple-element.11.same_ref, f32[256,128]{1,0:T(8,128)S(1)} %get-tuple-element.12.scale_ref, bf16[512,256]{1,0:T(8,128)(2,1)S(1)} %get-tuple-element.13.place_ref, bf16[8,384,128]{2,1,0:T(8,128)(2,1)S(1)} %all-to-all-done.x_ref), custom_call_target="tpu_custom_call" | custom-call | tf_op jit(solution)/shard_map/pallas_call | solution.py:223
  27.0 41.7 %all_to_all.15 = bf16[64,8,1152]{2,1,0:T(8,128)(2,1)S(1)} all-to-all(bf16[64,8,1152]{2,1,0:T(8,128)(2,1)S(1)} %bitcast.6), channel_id=1, replica_groups={{0,360,152,448,304,96,392,248,40,336,128,488,280,72,432,224,16,376,168,..., dimensions={0} | all-to-all | bytes 2359296 | tf_op jit(solution)/shard_map/all_to_all | solution.py:230
  68.6 0.5 shard_map.106
  69.1 14.9 %all_to_all.16.x_ref = bf16[8,96,384]{2,1,0:T(8,128)(2,1)S(1)} all-to-all(bf16[8,96,384]{2,1,0:T(8,128)(2,1)S(1)} %shard_map.106), channel_id=1, replica_groups=mesh['dp'=64,'tensor'=8] {'tensor'}, dimensions={0} | all-to-all | bytes 1179648 | tf_op jit(solution)/shard_map/all_to_all | solution.py:245
  84.0 0.8 shard_map.107
Async XLA Ops:
  2.8 10.4 %copy-start = (s32[8]{0:T(128)S(1)}, s32[8]{0:T(128)}, u32[]{:S(2)}) copy-start(s32[8]{0:T(128)} %weights_ref.1) | copy-start | bytes 100
  2.8 22.6 %all-to-all-start = ((bf16[8,384,128]{2,1,0:T(8,128)(2,1)}), bf16[8,384,128]{2,1,0:T(8,128)(2,1)S(1)}, u32[]{:S(2)}, u32[]{:S(2)}) async-start(bf16[8,384,128]{2,1,0:T(8,128)(2,1)} %shard_map.103), calls=%async_computation | async-start | bytes 1572864 | tf_op jit(solution)/shard_map/all_to_all | solution.py:209

commit v11 on v10

--- a/solution.py
+++ b/solution.py
@@ -16,8 +16,8 @@
 TN = (((0,), (0,)), ((), ()))
 
 LINE = 8
-STRIDE = 45
-UNSTRIDE = 37
+STRIDE = 13
+UNSTRIDE = 5
 
 PARAMS = pltpu.CompilerParams(vmem_limit_bytes=48 * 1024 * 1024)
 

time: 85.2 us -> 86.3 us (1.013); the launches traced: 84.8 us -> 84.8 us
    all_to_all x1, blocking collectives: 41.7 us -> 40.2 us  [local(): lax.all_to_all(in_slots.reshape(groups, PATCH_MAX, 3 * width), 'dp', spli...]
    all_to_all x1, blocking collectives: 14.9 us -> 16.3 us  [local(): lax.all_to_all(packed, 'tensor', split_axis=0, concat_axis=0, tiled=True)]
where the time goes in v11:
time: 86.3 us; the launch traced here: 84.8 us
  blocking collectives  56.4 us (65%)
  waiting for transfers between devices  10.7 us (12%)
  starting transfers between devices  10.3 us (12%)
  Pallas kernels  6.56 us (8%)
    all_to_all x1, blocking collectives, local(): lax.all_to_all(in_slots.reshape(groups, PATCH_MAX, 3 * width), 'dp', spli...  40.2 us
    all_to_all x1, blocking collectives, local(): lax.all_to_all(packed, 'tensor', split_axis=0, concat_axis=0, tiled=True)  16.3 us
    all_to_all x1, waiting for transfers between devices, local(): lax.all_to_all(by_rank, 'tensor', split_axis=0, concat_axis=0, tiled=True)  10.7 us
    all_to_all x1, starting transfers between devices, local(): lax.all_to_all(by_rank, 'tensor', split_axis=0, concat_axis=0, tiled=True)  10.3 us
    pallas_call x1, Pallas kernels, local(): pl.pallas_call(split_kernel, out_shape=jax.ShapeDtypeStruct((ranks, 4 * r...  2.18 us
  transfers between devices with their start and end apart: 1, of which 1 were waited for; matrix products, arithmetic and copies ran while one was open for 0% of the time, Pallas kernels for 2%

profile of v11, /device:TPU:1, one launch (start us, length us, event | category | flops | bytes accessed | tf_op | source)
XLA Modules:
  0.0 84.8 jit_solution(12782977889429758953)
XLA Ops:
  0.6 2.2 %shard_map.103 = bf16[8,384,128]{2,1,0:T(8,128)(2,1)} custom-call(bf16[32,3072]{1,0:T(8,128)(2,1)} %q_ref.1, bf16[32,3072]{1,0:T(8,128)(2,1)} %k_ref.1, bf16[32,3072]{1,0:T(8,128)(2,1)} %v_ref.1, bf16[32,3072]{1,0:T(8,128)(2,1)} %g_ref.1), custom_call_target="tpu_custom_call" | custom-call | tf_op jit(solution)/shard_map/pallas_call | solution.py:200
  2.8 0.0 copy-start
  2.8 10.3 %all-to-all-start = ((bf16[8,384,128]{2,1,0:T(8,128)(2,1)}), bf16[8,384,128]{2,1,0:T(8,128)(2,1)S(1)}, u32[]{:S(2)}, u32[]{:S(2)}) async-start(bf16[8,384,128]{2,1,0:T(8,128)(2,1)} %shard_map.103), calls=%async_computation | async-start | bytes 1572864 | tf_op jit(solution)/shard_map/all_to_all | solution.py:209
  13.2 0.0 copy-done
  13.2 1.6 %shard_map.104 = (f32[256,256]{1,0:T(8,128)S(1)}, f32[256,128]{1,0:T(8,128)S(1)}, bf16[512,256]{1,0:T(8,128)(2,1)S(1)}, bf16[256,512]{1,0:T(8,128)(2,1)S(1)}) custom-call(s32[1]{0:T(128)} %bitcast.at_ref, s32[32,64]{1,0:T(8,128)} %bitcast.8, s32[32,64]{1,0:T(8,128)} %bitcast.9, s32[32,64]{1,0:T(8,128)} %bitcast.10, s32[8]{0:T(128)S(1)} %copy-done), custom_call_target="tpu_custom_call" | custom-call | flops 16777216 | bytes 1048576 | tf_op jit(solution)/shard_map/pallas_call | solution.py:210
  14.7 10.7 %all-to-all-done.x_ref = bf16[8,384,128]{2,1,0:T(8,128)(2,1)S(1)} async-done(((bf16[8,384,128]{2,1,0:T(8,128)(2,1)}), bf16[8,384,128]{2,1,0:T(8,128)(2,1)S(1)}, u32[]{:S(2)}, u32[]{:S(2)}) %all-to-all-start) | async-done | bytes 786464 | tf_op jit(solution)/shard_map/all_to_all | solution.py:209
  25.5 1.5 %shard_map.105 = bf16[512,1152]{1,0:T(8,128)(2,1)S(1)} custom-call(f32[256,256]{1,0:T(8,128)S(1)} %get-tuple-element.11.same_ref, f32[256,128]{1,0:T(8,128)S(1)} %get-tuple-element.12.scale_ref, bf16[512,256]{1,0:T(8,128)(2,1)S(1)} %get-tuple-element.13.place_ref, bf16[8,384,128]{2,1,0:T(8,128)(2,1)S(1)} %all-to-all-done.x_ref), custom_call_target="tpu_custom_call" | custom-call | tf_op jit(solution)/shard_map/pallas_call | solution.py:223
  27.0 40.2 %all_to_all.15 = bf16[64,8,1152]{2,1,0:T(8,128)(2,1)S(1)} all-to-all(bf16[64,8,1152]{2,1,0:T(8,128)(2,1)S(1)} %bitcast.6), channel_id=1, replica_groups={{0,328,152,480,304,64,392,216,40,368,128,456,280,104,432,192,16,344,168..., dimensions={0} | all-to-all | bytes 2359296 | tf_op jit(solution)/shard_map/all_to_all | solution.py:230
  67.1 0.5 shard_map.106
  67.7 16.3 %all_to_all.16.x_ref = bf16[8,96,384]{2,1,0:T(8,128)(2,1)S(1)} all-to-all(bf16[8,96,384]{2,1,0:T(8,128)(2,1)S(1)} %shard_map.106), channel_id=1, replica_groups=mesh['dp'=64,'tensor'=8] {'tensor'}, dimensions={0} | all-to-all | bytes 1179648 | tf_op jit(solution)/shard_map/all_to_all | solution.py:245
  83.9 0.8 %shard_map.107 = (bf16[32,3072]{1,0:T(8,128)(2,1)}, bf16[32,3072]{1,0:T(8,128)(2,1)}, bf16[32,3072]{1,0:T(8,128)(2,1)}) custom-call(bf16[8,96,384]{2,1,0:T(8,128)(2,1)S(1)} %all_to_all.16.x_ref), custom_call_target="tpu_custom_call" | custom-call | tf_op jit(solution)/shard_map/pallas_call | solution.py:247
Async XLA Ops:
  2.8 10.4 %copy-start = (s32[8]{0:T(128)S(1)}, s32[8]{0:T(128)}, u32[]{:S(2)}) copy-start(s32[8]{0:T(128)} %weights_ref.1) | copy-start | bytes 100
  2.8 22.6 %all-to-all-start = ((bf16[8,384,128]{2,1,0:T(8,128)(2,1)}), bf16[8,384,128]{2,1,0:T(8,128)(2,1)S(1)}, u32[]{:S(2)}, u32[]{:S(2)}) async-start(bf16[8,384,128]{2,1,0:T(8,128)(2,1)} %shard_map.103), calls=%async_computation | async-start | bytes 1572864 | tf_op jit(solution)/shard_map/all_to_all | solution.py:209

commit v12 on v11

--- a/solution.py
+++ b/solution.py
@@ -16,8 +16,8 @@
 TN = (((0,), (0,)), ((), ()))
 
 LINE = 8
-STRIDE = 13
-UNSTRIDE = 5
+STRIDE = 27
+UNSTRIDE = 19
 
 PARAMS = pltpu.CompilerParams(vmem_limit_bytes=48 * 1024 * 1024)
 

time: 86.3 us -> 86.8 us (level)
  the two profiles are of different devices: /device:TPU:1 before, /device:TPU:8 now
where the time goes in v12:
time: 86.8 us; the launch traced here: 86.4 us
  blocking collectives  63.3 us (73%)
  waiting for transfers between devices  11.6 us (13%)
  Pallas kernels  6.57 us (8%)
  starting transfers between devices  4.31 us (5%)
    all_to_all x1, blocking collectives, local(): lax.all_to_all(in_slots.reshape(groups, PATCH_MAX, 3 * width), 'dp', spli...  49.8 us
    all_to_all x1, blocking collectives, local(): lax.all_to_all(packed, 'tensor', split_axis=0, concat_axis=0, tiled=True)  13.5 us
    all_to_all x1, waiting for transfers between devices, local(): lax.all_to_all(by_rank, 'tensor', split_axis=0, concat_axis=0, tiled=True)  11.6 us
    all_to_all x1, starting transfers between devices, local(): lax.all_to_all(by_rank, 'tensor', split_axis=0, concat_axis=0, tiled=True)  4.31 us
    pallas_call x1, Pallas kernels, local(): pl.pallas_call(split_kernel, out_shape=jax.ShapeDtypeStruct((ranks, 4 * r...  2.18 us
  transfers between devices with their start and end apart: 1, of which 1 were waited for; matrix products, arithmetic and copies ran while one was open for 0% of the time, Pallas kernels for 2%

profile of v12, /device:TPU:8, one launch (start us, length us, event | category | flops | bytes accessed | tf_op | source)
XLA Modules:
  0.0 86.4 jit_solution(17763276314740008532)
XLA Ops:
  0.6 2.2 %shard_map.103 = bf16[8,384,128]{2,1,0:T(8,128)(2,1)} custom-call(bf16[32,3072]{1,0:T(8,128)(2,1)} %q_ref.1, bf16[32,3072]{1,0:T(8,128)(2,1)} %k_ref.1, bf16[32,3072]{1,0:T(8,128)(2,1)} %v_ref.1, bf16[32,3072]{1,0:T(8,128)(2,1)} %g_ref.1), custom_call_target="tpu_custom_call" | custom-call | tf_op jit(solution)/shard_map/pallas_call | solution.py:200
  2.8 0.0 copy-start
  2.8 4.3 %all-to-all-start = ((bf16[8,384,128]{2,1,0:T(8,128)(2,1)}), bf16[8,384,128]{2,1,0:T(8,128)(2,1)S(1)}, u32[]{:S(2)}, u32[]{:S(2)}) async-start(bf16[8,384,128]{2,1,0:T(8,128)(2,1)} %shard_map.103), calls=%async_computation | async-start | bytes 1572864 | tf_op jit(solution)/shard_map/all_to_all | solution.py:209
  7.1 0.0 copy-done
  7.1 1.6 %shard_map.104 = (f32[256,256]{1,0:T(8,128)S(1)}, f32[256,128]{1,0:T(8,128)S(1)}, bf16[512,256]{1,0:T(8,128)(2,1)S(1)}, bf16[256,512]{1,0:T(8,128)(2,1)S(1)}) custom-call(s32[1]{0:T(128)} %bitcast.at_ref, s32[32,64]{1,0:T(8,128)} %bitcast.8, s32[32,64]{1,0:T(8,128)} %bitcast.9, s32[32,64]{1,0:T(8,128)} %bitcast.10, s32[8]{0:T(128)S(1)} %copy-done), custom_call_target="tpu_custom_call" | custom-call | flops 16777216 | bytes 1048576 | tf_op jit(solution)/shard_map/pallas_call | solution.py:210
  8.7 11.6 %all-to-all-done.x_ref = bf16[8,384,128]{2,1,0:T(8,128)(2,1)S(1)} async-done(((bf16[8,384,128]{2,1,0:T(8,128)(2,1)}), bf16[8,384,128]{2,1,0:T(8,128)(2,1)S(1)}, u32[]{:S(2)}, u32[]{:S(2)}) %all-to-all-start) | async-done | bytes 786464 | tf_op jit(solution)/shard_map/all_to_all | solution.py:209
  20.3 1.5 %shard_map.105 = bf16[512,1152]{1,0:T(8,128)(2,1)S(1)} custom-call(f32[256,256]{1,0:T(8,128)S(1)} %get-tuple-element.11.same_ref, f32[256,128]{1,0:T(8,128)S(1)} %get-tuple-element.12.scale_ref, bf16[512,256]{1,0:T(8,128)(2,1)S(1)} %get-tuple-element.13.place_ref, bf16[8,384,128]{2,1,0:T(8,128)(2,1)S(1)} %all-to-all-done.x_ref), custom_call_target="tpu_custom_call" | custom-call | tf_op jit(solution)/shard_map/pallas_call | solution.py:223
  21.8 49.8 %all_to_all.15 = bf16[64,8,1152]{2,1,0:T(8,128)(2,1)S(1)} all-to-all(bf16[64,8,1152]{2,1,0:T(8,128)(2,1)S(1)} %bitcast.6), channel_id=1, replica_groups={{0,216,432,80,296,448,160,376,24,240,392,104,256,472,184,336,48,200,416..., dimensions={0} | all-to-all | bytes 2359296 | tf_op jit(solution)/shard_map/all_to_all | solution.py:230
  71.6 0.5 shard_map.106
  72.1 13.5 %all_to_all.16.x_ref = bf16[8,96,384]{2,1,0:T(8,128)(2,1)S(1)} all-to-all(bf16[8,96,384]{2,1,0:T(8,128)(2,1)S(1)} %shard_map.106), channel_id=1, replica_groups=mesh['dp'=64,'tensor'=8] {'tensor'}, dimensions={0} | all-to-all | bytes 1179648 | tf_op jit(solution)/shard_map/all_to_all | solution.py:245
  85.6 0.8 shard_map.107
Async XLA Ops:
  2.8 4.3 %copy-start = (s32[8]{0:T(128)S(1)}, s32[8]{0:T(128)}, u32[]{:S(2)}) copy-start(s32[8]{0:T(128)} %weights_ref.1) | copy-start | bytes 100
  2.8 17.5 %all-to-all-start = ((bf16[8,384,128]{2,1,0:T(8,128)(2,1)}), bf16[8,384,128]{2,1,0:T(8,128)(2,1)S(1)}, u32[]{:S(2)}, u32[]{:S(2)}) async-start(bf16[8,384,128]{2,1,0:T(8,128)(2,1)} %shard_map.103), calls=%async_computation | async-start | bytes 1572864 | tf_op jit(solution)/shard_map/all_to_all | solution.py:209
